TPU v7x, 32 devices: a whole 2x2x4 slice. The times are simulated.
32 devices in a mesh: dp: 8 (over y, x, core), tensor: 4 (over z).
Axes of the slice: x: 2, y: 2, z: 4, core: 2. Of those that a mesh axis runs over, the one named last changes fastest.
Arguments:
- tokens: bfloat16 [8192, 1024], P(('dp', 'tensor')), may hold values from -6 to 6
- cotangent: bfloat16 [8192, 1024], P(('dp', 'tensor')), may hold values from -6 to 6
- segments: int32 [8, 1024], P('dp'), may hold values from 0 to 3, never falling along the last dimension, each value on 1 to 800 neighbouring positions
- norm_gains: bfloat16 [2, 1024], replicated, may hold values from 0.5 to 1.5
- mixer_in: bfloat16 [1024, 6144], P('dp', 'tensor'), may hold values from -0.1875 to 0.1875
- mixer_small: bfloat16 [2, 1024, 8], P(None, 'dp', 'tensor'), may hold values from -0.1875 to 0.1875
- conv_weight: bfloat16 [4, 8, 512], P(None, 'tensor', 'dp'), may hold values from -3 to 3
- head_params: float32 [2, 8], replicated, may hold values from -10 to 3, as said below
- out_norm: bfloat16 [8, 256], P('tensor', 'dp'), may hold values from 0.5 to 1.5
- mixer_out: bfloat16 [2048, 1024], P('tensor', 'dp'), may hold values from -0.125 to 0.125
- ffn_in: bfloat16 [2, 1024, 2816], P(None, 'dp', 'tensor'), may hold values from -0.1875 to 0.1875
- ffn_out: bfloat16 [2816, 1024], P('tensor', 'dp'), may hold values from -0.109375 to 0.109375
Outputs:
- output: bfloat16 [8192, 1024], P(('dp', 'tensor'))
- grad_tokens: float32 [8192, 1024], P(('dp', 'tensor'))
- grad_norm_gains: float32 [2, 1024], replicated
- grad_mixer_in: float32 [1024, 6144], P('dp', 'tensor')
- grad_mixer_small: float32 [2, 1024, 8], P(None, 'dp', 'tensor')
- grad_conv_weight: float32 [4, 8, 512], P(None, 'tensor', 'dp')
- grad_head_params: float32 [2, 8], replicated
- grad_out_norm: float32 [8, 256], P('tensor', 'dp')
- grad_mixer_out: float32 [2048, 1024], P('tensor', 'dp')
- grad_ffn_in: float32 [2, 1024, 2816], P(None, 'dp', 'tensor')
- grad_ffn_out: float32 [2816, 1024], P('tensor', 'dp')
Inputs may be any that keep to these rules, and one draw needn't show every extreme that they name: `segments`: within each sequence the numbers never fall; each document has 1 to 800 tokens and some document has exactly 800. `head_params`: row 0 is the logarithm of each head's decay rate, row 1 the bias added before the softplus.
All inputs are finite; a program needn't handle non-finite values.
Results may differ from a plain program's by a relative error of at most 0.019.
Values may be sent and summed in bfloat16 or wider, within the bound.
No kernel may reach another device: no remote copies, remote signals or barrier semaphores. Data moves between devices by JAX's collectives and lax.ppermute only.
A program may use at most 192 MiB of HBM per device.

v0:
```python
import functools
import jax
import jax.numpy as jnp
from jax import lax
from jax.experimental import pallas as pl
from jax.experimental.pallas import tpu as pltpu
from jax.sharding import PartitionSpec as P

DK = 128
DV = 256
MIX = 2 * DK + 2 * DV
CONV = 2 * DK + DV
CHUNK = 128
LANES = 128
TAPS = 4
BASE = 16
PER = 2
BACK = 2
PARTS = 2
BETA_AT = 8

NN = ((1,), (0,))
NT = ((1,), (1,))
TN = ((0,), (0,))

f32 = jnp.float32
bf16 = jnp.bfloat16


def dot(a, b, dims, passes):
    if passes == 6:
        return lax.dot_general(
            a, b, (dims, ((), ())), precision=lax.Precision.HIGHEST, preferred_element_type=f32
        )
    a_hi = a.astype(bf16)
    b_hi = b.astype(bf16)
    out = lax.dot_general(a_hi, b_hi, (dims, ((), ())), preferred_element_type=f32)
    if passes == 3:
        a_lo = (a - a_hi.astype(f32)).astype(bf16)
        b_lo = (b - b_hi.astype(f32)).astype(bf16)
        out = out + lax.dot_general(a_hi, b_lo, (dims, ((), ())), preferred_element_type=f32)
        out = out + lax.dot_general(a_lo, b_hi, (dims, ((), ())), preferred_element_type=f32)
    return out


def exact_left(mask, b):
    hi = b.astype(bf16)
    rest = b - hi.astype(f32)
    mid = rest.astype(bf16)
    low = (rest - mid.astype(f32)).astype(bf16)
    out = lax.dot_general(mask, hi, (NN, ((), ())), preferred_element_type=f32)
    out = out + lax.dot_general(mask, mid, (NN, ((), ())), preferred_element_type=f32)
    return out + lax.dot_general(mask, low, (NN, ((), ())), preferred_element_type=f32)


def sigmoid(x):
    return 1.0 / (1.0 + jnp.exp(-x))


def log1p(y):
    return jnp.where(y < 1e-4, y - 0.5 * y * y, jnp.log(1.0 + y))


def softplus(x):
    return jnp.maximum(x, 0.0) + log1p(jnp.exp(-jnp.abs(x)))


def iotas():
    shape = (CHUNK, CHUNK)
    return lax.broadcasted_iota(jnp.int32, shape, 0), lax.broadcasted_iota(jnp.int32, shape, 1)


def token_scalars(info, head_rows, heads):
    row, col = iotas()
    beta = sigmoid(info)
    rate = -jnp.exp(head_rows[0:1])
    pre = info + head_rows[1:2]
    g = rate * softplus(pre)
    total = exact_left((row >= col).astype(bf16), g)
    lane = lax.broadcasted_iota(jnp.int32, (CHUNK, LANES), 1)
    across = jnp.where(lane < BETA_AT, info, total).T
    return beta, g, pre, total, across


def head_scalars(h, heads, info, beta, total, across):
    row, col = iotas()
    at = BETA_AT + heads + h
    seg_col = info[:, 0:1]
    seg_row = across[0:1, :]
    tot_col = total[:, at : at + 1]
    tot_row = across[at : at + 1, :]
    keep = (seg_col == seg_row) & (row >= col)
    decay = jnp.exp(jnp.where(keep, tot_col - tot_row, -1e30))
    strict = jnp.where(row > col, decay, 0.0)
    beta_col = beta[:, BETA_AT + h : BETA_AT + h + 1]
    carried = jnp.exp(tot_col) * info[:, 7:8]
    last = CHUNK - 1
    end = jnp.where(
        seg_col == seg_col[last : last + 1], jnp.exp(tot_col[last : last + 1] - tot_col), 0.0
    )
    carried_last = carried[last : last + 1]
    return decay, strict, beta_col, carried, end, carried_last


def invert(lowers, passes):
    row, col = iotas()
    shape = (BASE, CHUNK)
    lane = lax.broadcasted_iota(jnp.int32, shape, 1)
    own = lax.broadcasted_iota(jnp.int32, shape, 0)
    start = lane // BASE * BASE
    blocks = CHUNK // BASE
    inside = [lane // BASE == b for b in range(blocks)]
    packs = []
    for lower in lowers:
        packed = jnp.zeros(shape, f32)
        for b in range(blocks):
            packed = jnp.where(inside[b], lower[b * BASE : (b + 1) * BASE], packed)
        packs.append(packed)
    invs = [jnp.where(own == lane % BASE, 1.0, 0.0)] * len(lowers)
    for j in range(BASE - 1):
        at = start + j
        invs = [
            inv - jnp.take_along_axis(packed, at, axis=1) * inv[j : j + 1]
            for inv, packed in zip(invs, packs)
        ]
    invs = [
        jnp.concatenate([jnp.where(inside[b], inv, 0.0) for b in range(blocks)], 0) for inv in invs
    ]
    size = BASE
    while size < CHUNK:
        part = ((row // (2 * size)) == (col // (2 * size))) & ((row // size) != (col // size))
        steps = [
            dot(jnp.where(part, lower, 0.0), inv, NN, passes) for lower, inv in zip(lowers, invs)
        ]
        invs = [inv - dot(inv, step, NN, passes) for inv, step in zip(invs, steps)]
        size *= 2
    return invs


def normalised(act):
    factor = lax.rsqrt(jnp.sum(act * act, -1, keepdims=True) + 1e-06)
    return act * factor, factor


def with_scalars(places, extra, heads):
    lane = lax.broadcasted_iota(jnp.int32, places.shape, 1)
    return jnp.where((lane >= BETA_AT) & (lane < BETA_AT + 2 * heads), extra, places)


def forward_body(
    heads, prec, places_ref, extra_ref, proj_ref, conv_ref, head_ref, onorm_ref, state_in_ref,
    tail_in_ref,
    *refs,
):
    (
        z_ref, mixed_ref, out_ref, delta_ref, across_ref, state_out_ref, solve_ref, kk_ref, qk_ref,
        state_ref, tail_ref,
    ) = refs[-11:]

    @pl.when(pl.program_id(0) == 0)
    def _():
        state_ref[...] = state_in_ref[...]
        tail_ref[...] = tail_in_ref[...]

    rows = PER * CHUNK
    ready = {}
    first = {}
    infos = [
        with_scalars(
            places_ref[u * CHUNK : (u + 1) * CHUNK],
            extra_ref[u * CHUNK : (u + 1) * CHUNK],
            heads,
        )
        for u in range(PER)
    ]
    scalars = [token_scalars(info, head_ref[...], heads) for info in infos]
    for h in range(heads):
        at = h * MIX
        cat = h * CONV
        part = proj_ref[:, at : at + CONV]
        ext = jnp.concatenate([tail_ref[:, cat : cat + CONV], part], 0)
        tail_ref[:, cat : cat + CONV] = part[rows - 8 :]
        mixed = conv_ref[TAPS - 1 : TAPS, cat : cat + CONV] * part
        for s in range(1, TAPS):
            shifted = ext[8 - s : 8 - s + rows]
            mixed = mixed + conv_ref[TAPS - 1 - s : TAPS - s, cat : cat + CONV] * jnp.where(
                places_ref[:, s : s + 1] > 0.5, shifted, 0.0
            )
        mixed_ref[:, cat : cat + CONV] = mixed
        act = mixed * sigmoid(mixed)
        queries, _ = normalised(act[:, :DK])
        queries = queries * DK ** (-0.5)
        keys, _ = normalised(act[:, DK : 2 * DK])
        for u in range(PER):
            own = slice(u * CHUNK, (u + 1) * CHUNK)
            query = queries[own]
            key = keys[own]
            value = act[own, 2 * DK :]
            beta, g, pre, total, across = scalars[u]
            decay, strict, beta_col, carried, end, carried_last = head_scalars(
                h, heads, infos[u], beta, total, across
            )
            inner = dot(jnp.concatenate([key, query], 0), key, NT, prec["kk"])
            kk = inner[:CHUNK]
            qk = inner[CHUNK:]
            kk_ref[u, h] = kk
            qk_ref[u, h] = qk
            first[u, h] = (
                beta_col * strict * kk,
                jnp.concatenate([beta_col * value, (beta_col * carried) * key], 1),
                carried * query, decay * qk, end * key, carried_last,
            )
    order = list(first)
    for at, inv in zip(order, invert([first[at][0] for at in order], prec["inv"])):
        u, h = at
        own = slice(u * CHUNK, (u + 1) * CHUNK)
        lower, sides, reads_q, attend, ends, carried_last = first[at]
        solve_ref[u, h] = inv
        solved = dot(inv, sides, NN, prec["solve"])
        across_ref[own, h * DK : (h + 1) * DK] = solved[:, DV:]
        ready[at] = (
            jnp.concatenate([reads_q, solved[:, DV:]], 0), solved[:, :DV], attend, ends,
            carried_last,
        )
    for u in range(PER):
        own = slice(u * CHUNK, (u + 1) * CHUNK)
        for h in range(heads):
            readers, fixed, attend, ends, carried_last = ready[u, h]
            state = state_ref[h]
            state_out_ref[u, h] = state
            reads = dot(readers, state, NN, prec["state"])
            delta = fixed - reads[CHUNK:]
            state_ref[h] = carried_last * state + dot(ends, delta, TN, prec["state"])
            result = reads[:CHUNK] + dot(attend, delta, NN, prec["attend"])
            delta_ref[own, h * DV : (h + 1) * DV] = delta
            out_ref[own, h * DV : (h + 1) * DV] = result
            gate = proj_ref[own, h * MIX + CONV : (h + 1) * MIX]
            factor = lax.rsqrt(jnp.mean(result * result, -1, keepdims=True) + 1e-05)
            z = result * factor * onorm_ref[:, h * DV : (h + 1) * DV] * (gate * sigmoid(gate))
            z_ref[own, h * DV : (h + 1) * DV] = z.astype(bf16)


def backward_body(
    heads, prec, places_ref, extra_ref, proj_ref, conv_ref, head_ref, onorm_ref,
    mixed_ref, out_ref, delta_ref, across_ref, state_in_ref, solve_ref, kk_ref, qk_ref, dz_ref,
    dstate_in_ref, lead_in_ref, dconv_in_ref, dhead_in_ref, donorm_in_ref,
    *refs,
):
    dproj_ref, dstate_ref, lead_ref, dconv_ref, dhead_ref, donorm_ref = refs[-6:]

    @pl.when(pl.program_id(0) == 0)
    def _():
        dstate_ref[...] = dstate_in_ref[...]
        lead_ref[...] = lead_in_ref[...]
        dconv_ref[...] = dconv_in_ref[...]
        dhead_ref[...] = dhead_in_ref[...]
        donorm_ref[...] = donorm_in_ref[...]

    row, col = iotas()
    lane = lax.broadcasted_iota(jnp.int32, (CHUNK, LANES), 1)
    from_here = (row <= col).astype(bf16)
    items = [(u, h) for u in reversed(range(BACK)) for h in range(heads)]
    rows_of = {u: slice(u * CHUNK, (u + 1) * CHUNK) for u in range(BACK)}
    infos = {
        u: with_scalars(places_ref[rows_of[u]], extra_ref[rows_of[u]], heads)
        for u in range(BACK)
    }
    scalars = {u: token_scalars(infos[u], head_ref[...], heads) for u in range(BACK)}
    made = {}
    for u, h in items:
        own = rows_of[u]
        cat = h * CONV
        at = h * MIX
        mixed = mixed_ref[own, cat : cat + CONV]
        msig = sigmoid(mixed)
        act = mixed * msig
        q_unit, q_factor = normalised(act[:, :DK])
        key, k_factor = normalised(act[:, DK : 2 * DK])
        value = act[:, 2 * DK :]
        beta, g, pre, total, across = scalars[u]
        decay, strict, beta_col, carried, end, carried_last = head_scalars(
            h, heads, infos[u], beta, total, across
        )
        result = out_ref[own, h * DV : (h + 1) * DV]
        gate = proj_ref[own, at + CONV : at + MIX]
        gsig = sigmoid(gate)
        silu = gate * gsig
        onorm = onorm_ref[:, h * DV : (h + 1) * DV]
        factor = lax.rsqrt(jnp.mean(result * result, -1, keepdims=True) + 1e-05)
        normed = result * factor
        dz = dz_ref[own, h * DV : (h + 1) * DV].astype(f32)
        dzn = dz * normed
        donorm_ref[:, h * DV : (h + 1) * DV] += jnp.sum(dzn * silu, 0, keepdims=True)
        dgate = dzn * onorm * (gsig * (1.0 + gate * (1.0 - gsig)))
        dproj_ref[own, at + CONV : at + MIX] = dgate.astype(bf16)
        dnormed = dz * onorm * silu
        dout = factor * (dnormed - normed * jnp.mean(dnormed * normed, -1, keepdims=True))
        through = dot(decay * qk_ref[u, h], dout, TN, prec["attend"])
        made[u, h] = (
            mixed, msig, q_unit, q_factor, key, k_factor, value, decay, strict, beta_col, carried,
            end, carried_last, dout, through,
        )
    chain = {}
    for u, h in items:
        own = rows_of[u]
        q_unit, key, carried, end, carried_last, dout, through = (
            made[u, h][i] for i in (2, 4, 10, 11, 12, 13, 14)
        )
        dnext = dstate_ref[h]
        ddelta = through + dot(end * key, dnext, NN, prec["state"])
        dstate_ref[h] = carried_last * dnext + dot(
            jnp.concatenate(
                [carried * (q_unit * DK ** (-0.5)), -across_ref[own, h * DK : (h + 1) * DK]], 0
            ),
            jnp.concatenate([dout, ddelta], 0),
            TN,
            prec["state"],
        )
        chain[u, h] = (dnext, ddelta)
    solved = {}
    for u, h in items:
        own = rows_of[u]
        dnext, ddelta = chain[u, h]
        delta = delta_ref[own, h * DV : (h + 1) * DV]
        state = state_in_ref[u, h]
        x = dot(solve_ref[u, h], ddelta, TN, prec["solve"])
        dend = dot(delta, dnext, NT, prec["big"])
        dcl = jnp.sum(jnp.sum(state * dnext, 0, keepdims=True), 1, keepdims=True)
        big = dot(
            jnp.concatenate([made[u, h][13], x], 0),
            jnp.concatenate([state, delta], 0),
            NT,
            prec["big"],
        )
        solved[u, h] = (x, dend, dcl, big)
    inner = {}
    for u, h in items:
        q_unit, key, decay, strict, beta_col = (made[u, h][i] for i in (2, 4, 7, 8, 9))
        x, dend, dcl, big = solved[u, h]
        query = q_unit * DK ** (-0.5)
        dqk = decay * big[:CHUNK, DK:]
        das = -strict * big[CHUNK:, DK:]
        bdas = beta_col * das
        rows = dot(jnp.concatenate([dqk, das], 0), key, NN, prec["kk"])
        cols = dot(
            jnp.concatenate([dqk, bdas], 0),
            jnp.concatenate([query, key], 0),
            TN,
            prec["kk"],
        )
        pairs = jnp.where(row > col, dqk * qk_ref[u, h] + bdas * kk_ref[u, h], 0.0)
        inner[u, h] = (rows, cols, exact_left(from_here, pairs))
    sums = {
        u: [jnp.zeros((CHUNK, LANES), f32) for _ in range(4)] for u in range(BACK)
    }
    dacts = {}
    for u, h in items:
        (
            mixed, msig, q_unit, q_factor, key, k_factor, value, decay, strict, beta_col, carried,
            end, carried_last, dout, through,
        ) = made[u, h]
        x, dend, dcl, big = solved[u, h]
        rows, cols, pairs = inner[u, h]
        query = q_unit * DK ** (-0.5)
        dqc = carried * big[:CHUNK, :DK]
        dq = rows[:CHUNK] + dqc
        dk_end = end * dend
        dkb_c = -carried * big[CHUNK:, :DK]
        dk_row_b = rows[CHUNK:] + dkb_c
        dk = beta_col * dk_row_b + cols + dk_end
        xv = x * value
        dbeta = jnp.sum(xv[:, :DK] + xv[:, DK:] + key * dk_row_b, -1, keepdims=True)
        reach = jnp.sum(query * dqc + key * (beta_col * dkb_c), -1, keepdims=True)
        leave = jnp.sum(key * dk_end, -1, keepdims=True)
        spans = jnp.sum(jnp.where(row > col, pairs, 0.0), -1, keepdims=True) + carried_last * dcl
        at_h = lane == BETA_AT + heads + h
        sums[u][0] = jnp.where(lane == BETA_AT + h, dbeta, sums[u][0])
        sums[u][1] = jnp.where(at_h, reach, sums[u][1])
        sums[u][2] = jnp.where(at_h, leave, sums[u][2])
        sums[u][3] = jnp.where(at_h, spans, sums[u][3])
        scale_q = DK ** (-0.5) * q_factor
        daq = scale_q * (dq - q_unit * jnp.sum(q_unit * dq, -1, keepdims=True))
        dak = k_factor * (dk - key * jnp.sum(key * dk, -1, keepdims=True))
        dact = jnp.concatenate([daq, dak, beta_col * x], 1)
        dacts[u, h] = dact * (msig * (1.0 + mixed * (1.0 - msig)))
    for h in range(heads):
        at = h * MIX
        cat = h * CONV
        dmixed = jnp.concatenate([dacts[u, h] for u in range(BACK)], 0)
        ext = jnp.concatenate([dmixed, lead_ref[:, cat : cat + CONV]], 0)
        lead_ref[:, cat : cat + CONV] = dmixed[:8]
        part = proj_ref[:, at : at + CONV]
        dpart = conv_ref[TAPS - 1 : TAPS, cat : cat + CONV] * dmixed
        dconv_ref[TAPS - 1 : TAPS, cat : cat + CONV] += jnp.sum(dmixed * part, 0, keepdims=True)
        for s in range(1, TAPS):
            shifted = jnp.where(
                places_ref[:, 3 + s : 4 + s] > 0.5, ext[s : s + BACK * CHUNK], 0.0
            )
            dpart = dpart + conv_ref[TAPS - 1 - s : TAPS - s, cat : cat + CONV] * shifted
            dconv_ref[TAPS - 1 - s : TAPS - s, cat : cat + CONV] += jnp.sum(
                shifted * part, 0, keepdims=True
            )
        dproj_ref[:, at : at + CONV] = dpart.astype(bf16)
    rate = -jnp.exp(head_ref[0:1])
    for u in range(BACK):
        beta, g, pre, total, across = scalars[u]
        dbeta_all, reach_all, leave_all, spans_all = sums[u]
        dg = spans_all + exact_left(from_here, reach_all)
        dg = dg + exact_left((row > col).astype(bf16), leave_all)
        dpre = dg * rate * sigmoid(pre)
        dsmall = dbeta_all * beta * (1.0 - beta) + dpre
        dproj_ref[rows_of[u], heads * MIX :] = dsmall.astype(bf16)
        dhead_ref[0:1] += jnp.sum(dg * g, 0, keepdims=True)
        dhead_ref[1:2] += jnp.sum(dpre, 0, keepdims=True)


PREC = {"kk": 3, "inv": 3, "solve": 3, "state": 3, "attend": 3, "big": 3}
BUDGET = 56 << 20


def whole(shape):
    return pl.BlockSpec(shape, lambda c: (0,) * len(shape))


def forward_start(heads):
    return [jnp.zeros((heads, DK, DV), f32), jnp.zeros((8, heads * CONV), f32)]


def mixer_forward(part, before, places, proj, conv, head_rows, onorm, carry, heads, prec=PREC):
    length = proj.shape[0]
    count = length // CHUNK
    steps = count // PER // PARTS
    first = part * steps
    chunk = lambda width: pl.BlockSpec((PER * CHUNK, width), lambda c: (first + c, 0))
    lanes = pl.BlockSpec((PER * CHUNK, LANES), lambda c: (first + c, heads * MIX // LANES))
    square = lambda rows, width: pl.BlockSpec(
        (PER, heads, rows, width), lambda c: (first + c, 0, 0, 0)
    )
    outs = pl.pallas_call(
        functools.partial(forward_body, heads, prec),
        grid=(steps,),
        in_specs=[chunk(LANES), lanes, chunk(heads * MIX)]
        + [whole(x.shape) for x in (conv, head_rows, onorm, *carry)]
        + [pl.BlockSpec(memory_space=pl.ANY)] * len(before),
        out_specs=[
            chunk(heads * DV), chunk(heads * CONV), chunk(heads * DV), chunk(heads * DV),
            chunk(heads * DK), square(DK, DV), square(CHUNK, CHUNK), square(CHUNK, CHUNK),
            square(CHUNK, CHUNK),
        ]
        + [whole(x.shape) for x in carry],
        out_shape=[
            jax.ShapeDtypeStruct((length, heads * DV), bf16),
            jax.ShapeDtypeStruct((length, heads * CONV), f32),
            jax.ShapeDtypeStruct((length, heads * DV), f32),
            jax.ShapeDtypeStruct((length, heads * DV), f32),
            jax.ShapeDtypeStruct((length, heads * DK), f32),
            jax.ShapeDtypeStruct((count, heads, DK, DV), f32),
            jax.ShapeDtypeStruct((count, heads, CHUNK, CHUNK), f32),
            jax.ShapeDtypeStruct((count, heads, CHUNK, CHUNK), f32),
            jax.ShapeDtypeStruct((count, heads, CHUNK, CHUNK), f32),
        ]
        + [jax.ShapeDtypeStruct(x.shape, f32) for x in carry],
        compiler_params=pltpu.CompilerParams(
            dimension_semantics=("arbitrary",), vmem_limit_bytes=BUDGET
        ),
        cost_estimate=pl.CostEstimate(
            flops=length * heads * 32000000, bytes_accessed=length * heads * 6000, transcendentals=0
        ),
        input_output_aliases={6 + len(carry) + i: i for i in range(len(before))},
        name="mixer_forward",
    )(places, proj, proj, conv, head_rows, onorm, *carry, *before)
    return outs[:-2], outs[-2:]


def backward_start(heads):
    return [
        jnp.zeros((heads, DK, DV), f32), jnp.zeros((8, heads * CONV), f32),
        jnp.zeros((TAPS, heads * CONV), f32), jnp.zeros((8, LANES), f32),
        jnp.zeros((1, heads * DV), f32),
    ]


def mixer_backward(
    part, before, places, proj, conv, head_rows, onorm, kept, dz, carry, heads, prec=PREC
):
    length = proj.shape[0]
    steps = length // (BACK * CHUNK) // PARTS
    last = part * steps + steps - 1
    chunk = lambda width: pl.BlockSpec((BACK * CHUNK, width), lambda c: (last - c, 0))
    lanes = pl.BlockSpec((BACK * CHUNK, LANES), lambda c: (last - c, heads * MIX // LANES))
    square = lambda rows, width: pl.BlockSpec(
        (BACK, heads, rows, width), lambda c: (last - c, 0, 0, 0)
    )
    dproj, *carry = pl.pallas_call(
        functools.partial(backward_body, heads, prec),
        grid=(steps,),
        in_specs=[chunk(LANES), lanes, chunk(heads * MIX)]
        + [whole(x.shape) for x in (conv, head_rows, onorm)]
        + [
            chunk(heads * CONV), chunk(heads * DV), chunk(heads * DV),
            chunk(heads * DK), square(DK, DV), square(CHUNK, CHUNK), square(CHUNK, CHUNK),
            square(CHUNK, CHUNK), chunk(heads * DV),
        ]
        + [whole(x.shape) for x in carry]
        + [pl.BlockSpec(memory_space=pl.ANY)] * len(before),
        out_specs=[chunk(heads * MIX + LANES)] + [whole(x.shape) for x in carry],
        out_shape=[jax.ShapeDtypeStruct((length, heads * MIX + LANES), bf16)]
        + [jax.ShapeDtypeStruct(x.shape, f32) for x in carry],
        compiler_params=pltpu.CompilerParams(
            dimension_semantics=("arbitrary",), vmem_limit_bytes=BUDGET
        ),
        cost_estimate=pl.CostEstimate(
            flops=length * heads * 48000000, bytes_accessed=length * heads * 7000, transcendentals=0
        ),
        input_output_aliases={7 + len(kept) + len(carry): 0} if before else {},
        name="mixer_backward",
    )(places, proj, proj, conv, head_rows, onorm, *kept, dz, *carry, *before)
    return dproj, carry


def token_places(segments):
    length = segments.shape[-1]
    seg = segments.reshape(length)
    columns = [seg.astype(f32)]
    for s in range(1, TAPS):
        before = jnp.concatenate([jnp.full((s,), -1, seg.dtype), seg[:-s]])
        columns.append((before == seg).astype(f32))
    for s in range(1, TAPS):
        beyond = jnp.concatenate([seg[s:], jnp.full((s,), -1, seg.dtype)])
        columns.append((beyond == seg).astype(f32))
    ends = seg.reshape(-1, CHUNK)[:, -1]
    ends = jnp.concatenate([jnp.full((1,), -1, seg.dtype), ends[:-1]])
    columns.append((jnp.repeat(ends, CHUNK) == seg).astype(f32))
    return jnp.pad(jnp.stack(columns, 1), ((0, 0), (0, LANES - len(columns))))


def head_lanes(head):
    heads = head.shape[1]
    return jnp.pad(head, ((0, 6), (BETA_AT + heads, LANES - BETA_AT - 2 * heads)))


def ffn_body(where, place_ref, rows_ref, cot_ref, *refs):
    w_refs = refs[:-5]
    gate_ref, up_ref, hidden_ref, back_ref, out_ref = refs[-5:]
    pieces = len(where[0])
    size = rows_ref.shape[1] // pieces

    def weight(p, which):
        parts = [w_refs[run[p][0]][run[p][1], which] for run in where]
        return parts[0] if len(parts) == 1 else jnp.concatenate(parts, 1)

    def columns(p):
        return pl.ds(pl.multiple_of((p ^ place_ref[0]) * size, size), size)

    def project(left_ref, which):
        total = None
        for p in range(pieces):
            part = lax.dot_general(
                left_ref[:, columns(p)], weight(p, which), (NT, ((), ())),
                preferred_element_type=f32,
            )
            total = part if total is None else total + part
        return total

    gate = project(rows_ref, 0)
    up = project(rows_ref, 1)
    grad_hidden = project(cot_ref, 2)
    sigma = sigmoid(gate)
    activ = gate * sigma
    hidden = (activ * up).astype(bf16)
    grad_gate = (grad_hidden * up * sigma * (1.0 + gate * (1.0 - sigma))).astype(bf16)
    grad_up = (grad_hidden * activ).astype(bf16)
    hidden_ref[...] = hidden
    gate_ref[...] = grad_gate
    up_ref[...] = grad_up
    for p in range(pieces):
        own = columns(p)
        back = lax.dot_general(
            grad_gate, weight(p, 0), (NN, ((), ())), preferred_element_type=f32
        )
        back = back + lax.dot_general(
            grad_up, weight(p, 1), (NN, ((), ())), preferred_element_type=f32
        )
        back_ref[:, own] = back.astype(bf16)
        out_ref[:, own] = lax.dot_general(
            hidden, weight(p, 2), (NN, ((), ())), preferred_element_type=f32
        ).astype(bf16)


FFN_TILE = 256


def ffn_both(place, rows, cot, weights, where):
    count, d = rows.shape
    hidden = weights[0].shape[2]
    tile = lambda width: pl.BlockSpec((FFN_TILE, width), lambda c, place: (c, 0))
    full = pl.BlockSpec(weights[0].shape, lambda c, place: (0, 0, 0, 0))
    return pl.pallas_call(
        functools.partial(ffn_body, where),
        grid_spec=pltpu.PrefetchScalarGridSpec(
            num_scalar_prefetch=1,
            grid=(count // FFN_TILE,),
            in_specs=[tile(d), tile(d)] + [full] * len(weights),
            out_specs=[tile(hidden), tile(hidden), tile(hidden), tile(d), tile(d)],
        ),
        out_shape=[
            jax.ShapeDtypeStruct((count, width), bf16) for width in (hidden, hidden, hidden, d, d)
        ],
        compiler_params=pltpu.CompilerParams(
            dimension_semantics=("arbitrary",), vmem_limit_bytes=BUDGET
        ),
        cost_estimate=pl.CostEstimate(
            flops=24 * count * d * hidden, bytes_accessed=8 * count * d, transcendentals=0
        ),
        name="ffn_both",
    )(place.reshape(1), rows, cot, *weights)


def ffn_grads_body(place_ref, rows_ref, cot_ref, gate_ref, up_ref, hidden_ref, *refs):
    out_refs = refs[:-1]
    flipped_ref = refs[-1]

    @pl.when(pl.program_id(0) == 0)
    def _():
        for i, ref in enumerate((gate_ref, up_ref, hidden_ref)):
            flipped_ref[i] = ref[...].T

    lanes = rows_ref.shape[1] // len(out_refs)
    for i, right in enumerate((rows_ref, rows_ref, cot_ref)):
        grad = lax.dot_general(
            flipped_ref[i], right[...], (NN, ((), ())), preferred_element_type=f32
        ).astype(bf16)
        for j, out_ref in enumerate(out_refs):
            out_ref[0, i] = grad[:, j * lanes : (j + 1) * lanes]


def ffn_weight_grads(place, rows, cot, gate, up, hidden, pieces, split):
    count, d = rows.shape
    width = hidden.shape[1]
    size = d // pieces
    column = pl.BlockSpec((count, size), lambda p, place: (0, p ^ place[0]))
    full = pl.BlockSpec((count, width), lambda p, place: (0, 0))
    return pl.pallas_call(
        ffn_grads_body,
        grid_spec=pltpu.PrefetchScalarGridSpec(
            num_scalar_prefetch=1,
            grid=(pieces,),
            in_specs=[column, column, full, full, full],
            out_specs=[
                pl.BlockSpec((1, 3, width, size // split), lambda p, place: (p, 0, 0, 0))
            ] * split,
            scratch_shapes=[pltpu.VMEM((3, width, count), bf16)],
        ),
        out_shape=[jax.ShapeDtypeStruct((pieces, 3, width, size // split), bf16)] * split,
        compiler_params=pltpu.CompilerParams(
            dimension_semantics=("arbitrary",), vmem_limit_bytes=BUDGET
        ),
        cost_estimate=pl.CostEstimate(
            flops=12 * count * d * width, bytes_accessed=8 * count * d, transcendentals=0
        ),
        name="ffn_weight_grads",
    )(place.reshape(1), rows, cot, gate, up, hidden)


def norm_factor(values):
    return lax.rsqrt(jnp.mean(values * values, -1, keepdims=True) + 1e-06)


def norm_backward(grad_out, scaled, factor, gain):
    grad_scaled = grad_out * gain
    grad_input = factor * (grad_scaled - scaled * jnp.mean(grad_scaled * scaled, -1, keepdims=True))
    return (grad_input, jnp.sum(grad_out * scaled, 0))


def product(left, right, dims):
    return lax.dot_general(left, right, (dims, ((), ())), preferred_element_type=f32)


def after(x, done):
    return lax.optimization_barrier((x, done))[0]


def exchange(x, axis, bit):
    return lax.ppermute(x, axis, [(i, i ^ bit) for i in range(lax.axis_size(axis))])


def sum_over(x, axis):
    ways = lax.axis_size(axis)
    if ways & (ways - 1):
        return lax.psum(x, axis)
    bit = 1
    while bit < ways:
        x = x + exchange(x, axis, bit)
        bit *= 2
    return x


def line_gather(x, axis, more=()):
    ways = lax.axis_size(axis)
    here = lax.axis_index(axis)
    up = [(i, i + 1) for i in range(ways - 1)]
    down = [(i + 1, i) for i in range(ways - 1)]
    below = [x]
    above = [x]
    for _ in range(ways - 1):
        below.append(lax.ppermute(below[-1], axis, up))
        above.append(lax.ppermute(above[-1], axis, down))
    below, above, more = lax.optimization_barrier((below, above, more))
    blocks = []
    for slot in range(ways):
        block = x
        for at in range(ways):
            if at != slot:
                block = jnp.where(here == at, below[at - slot] if at > slot else above[slot - at], block)
        blocks.append(block)
    return jnp.concatenate(blocks, 0), more


def line_scatter(x, axis, beside=None):
    ways = lax.axis_size(axis)
    here = lax.axis_index(axis)
    size = x.shape[0] // ways
    up = [(i, i + 1) for i in range(ways - 1)]
    down = [(i + 1, i) for i in range(ways - 1)]

    def block(slot):
        return lax.dynamic_slice_in_dim(x, slot * size, size, 0).astype(f32)

    low = None
    high = None
    other = None
    for k in range(1, ways):
        to_low = block(jnp.maximum(here - (ways - k), 0))
        to_high = block(jnp.minimum(here + (ways - k), ways - 1))
        if low is not None:
            to_low = to_low + low
            to_high = to_high + high
        low = lax.ppermute(to_low.astype(bf16), axis, down)
        high = lax.ppermute(to_high.astype(bf16), axis, up)
        if beside is not None:
            other = beside(k, other)
        low, high, other = lax.optimization_barrier((low, high, other))
        low = low.astype(f32)
        high = high.astype(f32)
    return block(here) + low + high, other


def shifted(x, axis, by):
    ways = lax.axis_size(axis)
    return lax.ppermute(x, axis, [(i, (i + by) % ways) for i in range(ways)])


def ordered(parts, axis):
    ways = len(parts)
    here = lax.axis_index(axis)
    blocks = []
    for slot in range(ways):
        block = parts[0]
        for at in range(ways):
            if at != slot:
                block = jnp.where(here == at, parts[(at - slot) % ways], block)
        blocks.append(block)
    return blocks


def swap_parts(block_to, axis):
    ways = lax.axis_size(axis)
    here = lax.axis_index(axis)
    parts = [block_to(here)]
    for s in range(1, ways):
        parts.append(shifted(block_to((here + s) % ways), axis, s))
    return parts


def swap_blocks(block_to, axis):
    return ordered(swap_parts(block_to, axis), axis)


class PlaneSum:

    def __init__(self, left, right):
        self.ways = lax.axis_size("dp")
        self.parts = ()
        if self.ways != 8:
            self.came = ()
            grad = product(left, right, TN).astype(bf16)
            self.total = lax.psum_scatter(grad, "dp", scatter_dimension=0, tiled=True).astype(f32)
            return
        core = lax.axis_index("dp") % 2
        self.size = left.shape[1] // self.ways
        blocks = [left[:, i * self.size : (i + 1) * self.size] for i in range(self.ways)]
        even = jnp.concatenate(blocks[::2], 1)
        odd = jnp.concatenate(blocks[1::2], 1)
        self.stay = jnp.where(core == 0, even, odd)
        self.right = right
        self.came = exchange(
            product(jnp.where(core == 0, odd, even), right, TN).astype(bf16), "dp", 1
        )

    def send(self):
        if self.ways == 8:
            total = product(self.stay, self.right, TN) + self.came.astype(f32)
            total = total.astype(bf16)
            place = lax.axis_index("dp") // 2
            block = lambda i: lax.dynamic_slice_in_dim(total, i * self.size, self.size, 0)
            self.total = block(place)
            self.parts = [exchange(block(place ^ (m // 2)), "dp", m) for m in (2, 4, 6)]

    def finish(self):
        total = self.total.astype(f32)
        for part in self.parts:
            total = total + part.astype(f32)
        return total


class OutWeights:

    def __init__(self, mixer_out):
        rows = mixer_out.T
        self.ways = lax.axis_size("dp")
        self.parts = ()
        self.rows = jnp.concatenate(swap_blocks(lambda i: rows, "tensor"), 1)

    def start(self, started):
        if self.ways == 8:
            rows = after(self.rows, started)
            self.parts = {m: exchange(rows, "dp", m) for m in (2, 4, 6)}

    def finish(self, done):
        if self.ways != 8:
            return lax.all_gather(self.rows, "dp", axis=0, tiled=True)
        here = lax.axis_index("dp")
        parts = dict(zip((2, 4, 6), after([self.parts[m] for m in (2, 4, 6)], done)))
        parts[0] = self.rows
        size = self.rows.shape[0]
        out = jnp.zeros((self.ways * size, self.rows.shape[1]), bf16)
        for m in (0, 2, 4, 6):
            parts[m + 1] = exchange(parts[m], "dp", 1)
        for m, part in parts.items():
            out = lax.dynamic_update_slice_in_dim(out, part, (here ^ m) * size, 0)
        return out

    def send_sum(self, total, width):
        return swap_parts(
            lambda i: lax.dynamic_slice_in_dim(total, i * width, width, 1), "tensor"
        )


class LineFfn:

    def __init__(self, ffn_in, ffn_out, started):
        self.own = jnp.stack([ffn_in[0].T, ffn_in[1].T, ffn_out])
        self.place = jnp.zeros((), jnp.int32)
        self.near = self.far = ()

    def middle(self, done, more):
        return done, more

    def plane_step(self):
        pass

    def finish(self, done):
        weights = lax.all_gather(self.own, "dp", axis=2, tiled=True)
        return (weights[None],)

    pieces = 1
    where = (((0, 0),),)

    def reach(self, x):
        return line_gather(x, "tensor")[0]

    def gather(self, x, far):
        return far

    def halves(self, x):
        return line_scatter(x, "tensor")[0], jnp.zeros((), bf16)

    def cross(self, far):
        return far

    def sum_start(self, grads):
        self.grads = grads

    def sum_step(self, done):
        return ()

    def sum_far(self, sent):
        pass

    def sum_finish(self):
        return lax.psum_scatter(self.grads[0][0], "dp", scatter_dimension=2, tiled=True)

    def send_sums(self, grads):
        return grads

    def own_grads(self, grads, came):
        return came.astype(f32)


TO_A = [(1, 0), (0, 2), (2, 3), (3, 1)]
TO_B = [(2, 1), (1, 2)]
BACK_A = [(0, 1), (2, 0), (3, 2), (1, 3)]
BACK_B = [(2, 1), (1, 2)]


class PairFfn:

    def __init__(self, ffn_in, ffn_out, started):
        self.core = lax.axis_index("dp") % 2
        self.here = lax.axis_index("tensor")
        self.place = lax.axis_index("dp") // 2
        self.own = after(jnp.stack([ffn_in[0].T, ffn_in[1].T, ffn_out]), started)
        self.a = lax.ppermute(self.own, "tensor", TO_A)
        self.b = lax.ppermute(self.own, "tensor", TO_B)

    def middle(self, done, more):
        here = self.here
        self.own, self.a, self.b, done, more = lax.optimization_barrier(
            (self.own, self.a, self.b, done, more)
        )
        own, a, b = self.own, self.a, self.b
        first = jnp.where(here == 0, own, jnp.where(here == 1, b, a))
        second = jnp.where(here == 3, own, jnp.where(here == 2, b, a))
        mine = jnp.where(self.core == 0, first, second)
        got = exchange(jnp.where(self.core == 0, second, first), "dp", 1)
        self.low = jnp.where(self.core == 0, mine, got)
        self.high = jnp.where(self.core == 0, got, mine)
        done = after(done, (self.low, self.high))
        self.near = exchange(self.low, "dp", 2), exchange(self.high, "dp", 4)
        return done, more

    def plane_step(self):
        self.low = jnp.stack([self.low, self.near[0]])
        self.high = jnp.stack([self.high, self.near[1]])
        self.far = exchange(self.low, "dp", 4), exchange(self.high, "dp", 2)

    def finish(self, done):
        far = after(self.far, done)
        return (self.low, far[0], self.high, far[1])

    pieces = 4
    where = (((0, 0), (0, 1), (1, 0), (1, 1)), ((2, 0), (3, 0), (2, 1), (3, 1)))

    def reach(self, x):
        return exchange(x, "tensor", 1)

    def gather(self, x, far):
        return jnp.concatenate([x, exchange(x, "dp", 1), far, exchange(far, "dp", 1)], 0)

    def halves(self, x):
        size = x.shape[0] // 4
        parts = [x[i * size : (i + 1) * size] for i in range(4)]
        far = (parts[2].astype(f32) + exchange(parts[3], "dp", 1).astype(f32)).astype(bf16)
        return parts[0].astype(f32) + exchange(parts[1], "dp", 1).astype(f32), far

    def cross(self, far):
        return exchange(far, "tensor", 1)

    def sum_start(self, grads):
        self.grads = grads
        low, high = grads
        across_x = jnp.stack([low[1], low[3]])
        self.near = exchange(across_x, "dp", 2), exchange(high[2:], "dp", 4)

    def sum_step(self, done):
        low, high = self.grads
        came = after(self.near, done)
        add = lambda x, y: (x.astype(f32) + y.astype(f32)).astype(bf16)
        self.kept = add(low[0], came[0][0]), add(high[0], came[1][0])
        return add(low[2], came[0][1]), add(high[1], came[1][1])

    def sum_far(self, sent):
        self.far = exchange(sent[0], "dp", 4), exchange(sent[1], "dp", 2)

    def sum_finish(self):
        came = self.far
        add = lambda x, y: (x.astype(f32) + y.astype(f32)).astype(bf16)
        low = add(self.kept[0], came[0])
        high = add(self.kept[1], came[1])
        core = self.core
        mine = jnp.where(core == 0, low, high)
        got = exchange(jnp.where(core == 0, high, low), "dp", 1)
        return jnp.where(core == 0, mine, got), jnp.where(core == 0, got, mine)

    def send_sums(self, sums):
        first, second = sums
        here = self.here
        a = lax.ppermute(jnp.where(here < 2, second, first), "tensor", BACK_A)
        b = lax.ppermute(jnp.where(here == 2, second, first), "tensor", BACK_B)
        return a, b

    def own_grads(self, sums, came):
        first, second = sums
        a, b = came
        here = self.here
        other = jnp.where(here == 0, first, jnp.where(here == 3, second, b))
        return a.astype(f32) + other.astype(f32)


CONV_AT = 64


def column_blocks(value, rows):
    ways, size = value.shape
    lanes = -(-size // rows)
    value = jnp.pad(value, ((0, 0), (0, lanes * rows - size)))
    return value.reshape(ways, lanes, rows).swapaxes(1, 2).reshape(ways * rows, lanes)


def from_columns(columns, shape, dim, rows):
    ways = columns.shape[0] // rows
    size = 1
    for extent in shape:
        size *= extent
    value = columns.reshape(ways, rows, -1).swapaxes(1, 2).reshape(ways, -1)[:, :size]
    value = jnp.moveaxis(value.reshape((ways,) + shape), 0, dim)
    return value.reshape(shape[:dim] + (ways * shape[dim],) + shape[dim + 1 :])


def lanes_of(small, conv, onorm):
    rows, width = small.shape
    used = BETA_AT + width
    rest = LANES - CONV_AT - conv.shape[1] - onorm.shape[1]
    zeros = lambda lanes: jnp.zeros((rows, lanes), small.dtype)
    return jnp.concatenate(
        [zeros(BETA_AT), small, zeros(CONV_AT - used), conv, onorm, zeros(rest)], 1
    )


def fetch_mixer(mixer_in, mixer_small, conv_weight, out_norm):
    rows, width = mixer_in.shape
    small = jnp.moveaxis(mixer_small, 0, 1).reshape(rows, -1)
    conv = column_blocks(conv_weight.reshape(1, -1), rows)
    onorm = column_blocks(out_norm.reshape(1, -1), rows)
    extended = jnp.concatenate([mixer_in, lanes_of(small, conv, onorm)], 1)
    w_in = lax.all_gather(extended, "dp", axis=0, tiled=True)
    at = width + CONV_AT
    w_conv = from_columns(w_in[:, at : at + conv.shape[1]], conv_weight.shape, 2, rows)
    at += conv.shape[1]
    w_onorm = from_columns(w_in[:, at : at + onorm.shape[1]], out_norm.shape, 1, rows)
    return w_in, w_conv, w_onorm


def shards(
    tokens, cotangent, segments, norm_gains, mixer_in, mixer_small, conv_weight, head_params,
    out_norm, mixer_out, ffn_in, ffn_out,
):
    heads = mixer_in.shape[1] // MIX
    all_heads = head_params.shape[1]
    ways = lax.axis_size("dp")
    teams = lax.axis_size("tensor")
    head_start = lax.axis_index("tensor") * heads
    head_local = lax.dynamic_slice_in_dim(head_params, head_start, heads, 1)
    gains = norm_gains.astype(f32)
    own = tokens.shape[0]
    inputs = tokens.astype(f32)
    factor_one = norm_factor(inputs)
    scaled_one = inputs * factor_one
    normed_one = (scaled_one * gains[0]).astype(bf16)
    out_weights = OutWeights(mixer_out)
    w_in, w_conv, w_onorm = fetch_mixer(mixer_in, mixer_small, conv_weight, out_norm)
    conv_rows = w_conv.astype(f32).reshape(TAPS, heads * CONV)
    onorm_row = w_onorm.astype(f32).reshape(1, heads * DV)
    head_rows = head_lanes(head_local)
    places = token_places(segments)
    rows_one, (out_weights.rows, constants, places) = line_gather(
        normed_one, "tensor", (out_weights.rows, (conv_rows, head_rows, onorm_row), places)
    )
    out_weights.start(rows_one)
    kind = PairFfn if teams == 4 and ways == 8 else LineFfn
    ffn = kind(ffn_in, ffn_out, rows_one)
    wide = heads * MIX
    proj = product(rows_one, w_in, NN)
    carry = forward_start(heads)
    made = []
    for part in range(PARTS):
        made, carry = mixer_forward(part, made, places, proj, *constants, carry, heads)
        if part == 0:
            carry, (cotangent, out_weights.parts) = ffn.middle(
                carry, (cotangent, out_weights.parts)
            )
            cot_far = ffn.reach(cotangent)
    mixed, *kept = made
    mixed, cot_far, ffn.near = lax.optimization_barrier((mixed, cot_far, ffn.near))
    ffn.plane_step()
    came = swap_parts(lambda i: lax.dynamic_slice_in_dim(mixed, i * own, own, 0), "tensor")
    out_t = out_weights.finish(came[-1])
    grad_rows = ffn.gather(cotangent, after(cot_far, came[-1]))
    mixed = jnp.concatenate(ordered(came, "tensor"), 1)
    middle = inputs + product(mixed, out_t, NT)
    factor_two = norm_factor(middle)
    scaled_two = middle * factor_two
    normed_two = (scaled_two * gains[1]).astype(bf16)
    rows_two = ffn.gather(normed_two, ffn.reach(normed_two))
    w_ffn = ffn.finish(normed_two)
    grad_gate, grad_up, hidden, back, forth = ffn_both(
        ffn.place, rows_two, grad_rows, w_ffn, ffn.where
    )
    grad_normed_two, far = ffn.halves(back)
    ffn_grads = ffn_weight_grads(
        ffn.place, after(rows_two, far), grad_rows, grad_gate, grad_up, hidden,
        ffn.pieces, len(ffn.where),
    )
    far, ffn_grads = lax.optimization_barrier((ffn.cross(far), ffn_grads))
    grad_normed_two = grad_normed_two + far.astype(f32)
    ffn.sum_start(ffn_grads)
    grad_middle_norm, grad_gain_two = norm_backward(
        grad_normed_two, scaled_two, factor_two, gains[1]
    )
    grad_middle = cotangent.astype(f32) + grad_middle_norm
    branch_grad = grad_middle.astype(bf16)
    grad_mixed = product(branch_grad, out_t, NN).astype(bf16)
    width = heads * DV
    came = swap_parts(
        lambda i: lax.dynamic_slice_in_dim(grad_mixed, i * width, width, 1), "tensor"
    )
    branch_grad, forth, near = after((branch_grad, forth, ffn.near), grad_mixed)
    ffn.near = near
    out_sum = PlaneSum(branch_grad, mixed)
    result, far = ffn.halves(forth)
    came, far, sums = lax.optimization_barrier((came, far, ffn.sum_step(grad_mixed)))
    ffn.sum_far(sums)
    result = result, ffn.cross(far)
    grad_mixed = jnp.concatenate(ordered(came, "tensor"), 0)
    carry = backward_start(heads)
    grad_proj = []
    for part in reversed(range(PARTS)):
        dproj, carry = mixer_backward(
            part, grad_proj, places, proj, *constants, kept, grad_mixed, carry, heads
        )
        grad_proj = [dproj]
        if part == PARTS - 1:
            carry, result, ffn.far, out_sum.came = lax.optimization_barrier(
                (carry, result, ffn.far, out_sum.came)
            )
            out_sum.send()
            ffn_sums = ffn.sum_finish()
            carry = after(carry, ffn_sums)
            ffn_came = ffn.send_sums(ffn_sums)
    grad_proj, ffn_came, out_sum.parts = lax.optimization_barrier(
        (dproj, ffn_came, out_sum.parts)
    )
    grad_conv, grad_head, grad_onorm = carry[2:]
    result = middle + result[0] + result[1].astype(f32)
    sent = product(grad_proj, w_in, NT).astype(bf16)
    grad_normed_one = lax.psum_scatter(
        sent, "tensor", scatter_dimension=0, tiled=True
    ).astype(f32)
    grad_proj = after(grad_proj, sent)
    grad_in = PlaneSum(rows_one, grad_proj[:, :wide])
    grad_in.send()
    head_full = lax.dynamic_update_slice_in_dim(
        jnp.zeros((2, all_heads), f32),
        grad_head[:2, BETA_AT + heads : BETA_AT + 2 * heads],
        head_start,
        1,
    )
    d = gains.shape[1]
    sizes = [2 * d + 2 * all_heads, grad_conv.size, grad_onorm.size, 2 * heads * d]
    ends = [sum(sizes[:i]) for i in range(5)]
    at = BETA_AT + 2 * heads
    grad_small = product(rows_one, grad_proj[:, wide:], TN)[:, BETA_AT:at]
    again = after(sent, grad_in.total)
    gain_one = jnp.sum(again.astype(f32) * rows_one.astype(f32), 0) / gains[0]
    parts = [
        gain_one, grad_gain_two, head_full.reshape(-1), grad_conv.reshape(-1),
        grad_onorm.reshape(-1), grad_small.T.reshape(-1),
    ]
    totals = sum_over(jnp.concatenate(parts), "dp")
    shared = totals[: sizes[0]]
    shared = sum(ordered(swap_parts(lambda i: shared, "tensor"), "tensor"))
    grad_in.parts, out_parts = lax.optimization_barrier(
        (grad_in.parts, out_sum.finish().astype(bf16))
    )
    out_out = sum(block.astype(f32) for block in out_weights.send_sum(out_parts, width))
    conv_total, onorm_total, small_total = (totals[ends[i] : ends[i + 1]] for i in (1, 2, 3))
    place = lax.axis_index("dp")

    def own_part(total, shape):
        size = shape[-1] // ways
        return lax.dynamic_slice_in_dim(total.reshape(shape), place * size, size, len(shape) - 1)

    out_conv = own_part(conv_total, (TAPS, heads, CONV))
    out_onorm = own_part(onorm_total, (heads, DV))
    out_small = own_part(small_total, (2, heads, d)).swapaxes(1, 2)
    totals = shared
    out_in = grad_in.finish()
    ffn_grads = ffn.own_grads(ffn_sums, ffn_came)
    grad_scaled = grad_normed_one * gains[0]
    grad_tokens = grad_middle + factor_one * (
        grad_scaled - scaled_one * jnp.mean(grad_scaled * scaled_one, -1, keepdims=True)
    )
    return (
        result.astype(bf16),
        grad_tokens,
        totals[: 2 * d].reshape(2, d),
        out_in,
        out_small,
        out_conv,
        totals[2 * d :].reshape(2, all_heads),
        out_onorm,
        out_out.T,
        ffn_grads[:2].swapaxes(1, 2),
        ffn_grads[2],
    )


def solution(mesh):
    in_specs = (
        P(("dp", "tensor"), None),
        P(("dp", "tensor"), None),
        P("dp", None),
        P(),
        P("dp", "tensor"),
        P(None, "dp", "tensor"),
        P(None, "tensor", "dp"),
        P(),
        P("tensor", "dp"),
        P("tensor", "dp"),
        P(None, "dp", "tensor"),
        P("tensor", "dp"),
    )
    out_specs = (
        P(("dp", "tensor"), None),
        P(("dp", "tensor"), None),
        P(),
        P("dp", "tensor"),
        P(None, "dp", "tensor"),
        P(None, "tensor", "dp"),
        P(),
        P("tensor", "dp"),
        P("tensor", "dp"),
        P(None, "dp", "tensor"),
        P("tensor", "dp"),
    )
    return jax.shard_map(shards, mesh=mesh, in_specs=in_specs, out_specs=out_specs, check_vma=False)
```

profile of v0, /device:TPU:0, one launch (start us, length us, event | category | flops | bytes accessed | tf_op | source)
XLA Modules:
  0.0 394.6 jit_solution(9372549600219819773)
XLA Ops:
  13.9 5.0 %collective-permute-start = (bf16[256,1024]{1,0:T(8,128)(2,1)S(1)}, bf16[256,1024]{1,0:T(8,128)(2,1)S(1)}, u32[]{:S(2)}, u32[]{:S(2)}) collective-permute-start(bf16[256,1024]{1,0:T(8,128)(2,1)S(1)} %fusion.10), channel_id=1, source_target_pairs={{0,1},{1,2},{2,3},{4,5},{5,6},{6,7},{8,9},{9,10},{10,11},{12,13},{... | collective-permute-start | bytes 1572872 | tf_op jit(solution)/shard_map/ppermute | solution.py:706
  20.2 4.7 %collective-permute-start.6 = (bf16[128,512]{0,1:T(8,128)(2,1)S(1)}, bf16[128,512]{0,1:T(8,128)(2,1)S(1)}, u32[]{:S(2)}, u32[]{:S(2)}) collective-permute-start(bf16[128,512]{0,1:T(8,128)(2,1)S(1)} %bitcast.124), channel_id=1, source_target_pairs={{0,3},{1,0},{2,1},{3,2},{4,7},{5,4},{6,5},{7,6},{8,11},{9,8},{10,9... | collective-permute-start | bytes 393224 | tf_op jit(solution)/shard_map/ppermute | solution.py:750
  26.7 4.5 %collective-permute-done = bf16[256,1024]{1,0:T(8,128)(2,1)S(1)} collective-permute-done((bf16[256,1024]{1,0:T(8,128)(2,1)S(1)}, bf16[256,1024]{1,0:T(8,128)(2,1)S(1)}, u32[]{:S(2)}, u32[]{:S(2)}) %collective-permute-start) | collective-permute-done | bytes 524320 | tf_op jit(solution)/shard_map/ppermute | solution.py:706
  31.2 9.5 %collective-permute-start.1 = (bf16[256,1024]{1,0:T(8,128)(2,1)S(1)}, bf16[256,1024]{1,0:T(8,128)(2,1)}, u32[]{:S(2)}, u32[]{:S(2)}) collective-permute-start(bf16[256,1024]{1,0:T(8,128)(2,1)S(1)} %collective-permute-done), channel_id=1, source_target_pairs={{0,1},{1,2},{2,3},{4,5},{5,6},{6,7},{8,9},{9,10},{10,11},{12,13},{... | collective-permute-start | bytes 1572872 | tf_op jit(solution)/shard_map/ppermute | solution.py:706
  49.8 7.0 %collective-permute-start.2 = (bf16[256,1024]{1,0:T(8,128)(2,1)}, bf16[256,1024]{1,0:T(8,128)(2,1)}, u32[]{:S(2)}, u32[]{:S(2)}) collective-permute-start(bf16[256,1024]{1,0:T(8,128)(2,1)} %collective-permute-done.1), channel_id=1, source_target_pairs={{0,1},{1,2},{2,3},{4,5},{5,6},{6,7},{8,9},{9,10},{10,11},{12,13},{... | collective-permute-start | bytes 1572872 | tf_op jit(solution)/shard_map/ppermute | solution.py:706
  62.1 4.5 %collective-permute-done.2 = bf16[256,1024]{1,0:T(8,128)(2,1)} collective-permute-done((bf16[256,1024]{1,0:T(8,128)(2,1)}, bf16[256,1024]{1,0:T(8,128)(2,1)}, u32[]{:S(2)}, u32[]{:S(2)}) %collective-permute-start.2) | collective-permute-done | bytes 524320 | tf_op jit(solution)/shard_map/ppermute | solution.py:706
  66.6 5.0 %collective-permute-done.5 = bf16[256,1024]{1,0:T(8,128)(2,1)} collective-permute-done((bf16[256,1024]{1,0:T(8,128)(2,1)}, bf16[256,1024]{1,0:T(8,128)(2,1)}, u32[]{:S(2)}, u32[]{:S(2)}) %collective-permute-start.5) | collective-permute-done | bytes 524320 | tf_op jit(solution)/shard_map/ppermute | solution.py:707
  80.9 5.9 %fusion.50.extra_ref.proj_ref = f32[1024,1664]{1,0:T(8,128)} fusion(bf16[1024,1024]{1,0:T(8,128)(2,1)S(1)} %pad_maximum_fusion, bf16[1024,1664]{1,0:T(8,128)(2,1)S(1)} %copy-done.75), kind=kOutput, calls=%fused_computation.177 | convolution fusion | flops 3489660928 | bytes 12320768 | tf_op jit(solution)/shard_map/dot_general | solution.py:676
  88.2 13.9 %mixer_forward.2 = (bf16[1024,512]{1,0:T(8,128)(2,1)}, f32[1024,1024]{1,0:T(8,128)}, f32[1024,512]{1,0:T(8,128)}, f32[1024,512]{1,0:T(8,128)}, f32[1024,256]{1,0...) custom-call(f32[1024,128]{1,0:T(8,128)} %pad.18.places_ref, ...), custom_call_target="tpu_custom_call" | custom-call | flops 65536000000 | bytes 12288000 | tf_op jit(solution)/shard_map/mixer_forward/pallas_call | solution.py:439
  110.1 13.9 %mixer_forward.3 = (bf16[1024,512]{1,0:T(8,128)(2,1)}, f32[1024,1024]{1,0:T(8,128)}, f32[1024,512]{1,0:T(8,128)}, f32[1024,512]{1,0:T(8,128)}, f32[1024,256]{1,0...) custom-call(f32[1024,128]{1,0:T(8,128)} %pad.18.places_ref, ...), custom_call_target="tpu_custom_call", output_to_operand_aliasing={{0}: (8, {}), {1}: (9, {}), {2}: (10, {}), {3}: (11, {}), {... | custom-call | flops 65536000000 | bytes 12288000 | tf_op jit(solution)/shard_map/mixer_forward/pallas_call | solution.py:439
  135.9 15.8 %collective-permute-done.19 = bf16[256,512]{1,0:T(8,128)(2,1)S(1)} collective-permute-done((bf16[256,512]{1,0:T(8,128)(2,1)S(1)}, bf16[256,512]{1,0:T(8,128)(2,1)S(1)}, u32[]{:S(2)}, u32[]{:S(2)}) %collective-permute-start.19) | collective-permute-done | bytes 262176 | tf_op jit(solution)/shard_map/ppermute | solution.py:750
  159.2 13.4 %collective-permute-done.26 = bf16[256,1024]{1,0:T(8,128)(2,1)S(1)} collective-permute-done((bf16[256,1024]{1,0:T(8,128)(2,1)S(1)}, bf16[256,1024]{1,0:T(8,128)(2,1)S(1)}, u32[]{:S(2)}, u32[]{:S(2)}) %collective-permute-start.26) | collective-permute-done | bytes 524320 | tf_op jit(solution)/shard_map/ppermute | solution.py:684
  174.9 6.2 %collective-permute-done.31.refs_3_ = bf16[2,3,704,128]{3,2,1,0:T(8,128)(2,1)} collective-permute-done((bf16[2,3,704,128]{3,2,1,0:T(8,128)(2,1)}, bf16[2,3,704,128]{3,2,1,0:T(8,128)(2,1)}, u32[]{:S(2)}, u32[]{:S(2)}) %collective-permute-start.31) | collective-permute-done | bytes 1081376 | tf_op jit(solution)/shard_map/ppermute | solution.py:684
  183.9 15.7 %ffn_both.1 = (bf16[1024,704]{1,0:T(8,128)(2,1)}, bf16[1024,704]{1,0:T(8,128)(2,1)}, bf16[1024,704]{1,0:T(8,128)(2,1)}, bf16[1024,1024]{1,0:T(8,128)(2,1)}, bf16[1024,1024]{1,0:T(8,128)(2,1)}) custom-call(s32[1]{0:T(128)} %bitcast.34.place_ref, bf16[1024,1024]{1,0:T(8,128)(2,1)} %pad_maximum_fusion.1.rows_ref, bf16[1024,1024]{1,0:T(8,128)(2,1)} %copy-done.73, ...), custom_call_target="tpu_custom_call" | custom-call | flops 17716740096 | bytes 8388608 | tf_op jit(solution)/shard_map/ffn_both/pallas_call | solution.py:598
  205.6 10.7 %ffn_weight_grads.1 = (bf16[4,3,704,128]{3,2,1,0:T(8,128)(2,1)}, bf16[4,3,704,128]{3,2,1,0:T(8,128)(2,1)}) custom-call(s32[1]{0:T(128)} %bitcast.34.place_ref, bf16[1024,1024]{1,0:T(8,128)(2,1)} %pad_maximum_fusion.1.rows_ref, bf16[1024,1024]{1,0:T(8,128)(2,1)} %copy-done.73, bf16[1024,704]{1,0:T(8,128)(2,1)} %get-tuple-element.182.gate_ref, ...), custom_call_target="tpu_custom_call" | custom-call | flops 8858370048 | bytes 8388608 | tf_op jit(solution)/shard_map/ffn_weight_grads/pallas_call | solution.py:643
  232.5 14.5 %collective-permute-done.38 = bf16[2,3,704,128]{3,2,1,0:T(8,128)(2,1)S(1)} collective-permute-done((bf16[2,3,704,128]{3,2,1,0:T(8,128)(2,1)S(1)}, bf16[2,3,704,128]{3,2,1,0:T(8,128)(2,1)S(1)}, u32[]{:S(2)}, u32[]{:S(2)}) %collective-permute-start.38) | collective-permute-done | bytes 1081376 | tf_op jit(solution)/shard_map/ppermute | solution.py:684
  259.8 15.5 %mixer_backward.2 = (bf16[1024,1664]{1,0:T(8,128)(2,1)}, f32[2,128,256]{2,1,0:T(8,128)}, f32[8,1024]{1,0:T(8,128)}, f32[4,1024]{1,0:T(4,128)}, f32[8,128]{1,0:T(8,128)}, /*index=5*/f32[1,512]{1,0:T(1,128)}) custom-call(f32[1024,128]{1,0:T(8,128)} %pad.18.places_ref, f32[1024,1664]{1,0:T(8,128)} %fusion.50.extra_ref.proj_ref, ...), custom_call_target="tpu_custom_call" | custom-call | flops 98304000000 | bytes 14336000 | tf_op jit(solution)/shard_map/mixer_backward/pallas_call | solution.py:494
  285.6 15.7 %mixer_backward.3 = (bf16[1024,1664]{1,0:T(8,128)(2,1)}, f32[2,128,256]{2,1,0:T(8,128)}, f32[8,1024]{1,0:T(8,128)}, f32[4,1024]{1,0:T(4,128)}, f32[8,128]{1,0:T(8,128)}, /*index=5*/f32[1,512]{1,0:T(1,128)}) custom-call(f32[1024,128]{1,0:T(8,128)} %pad.18.places_ref, f32[1024,1664]{1,0:T(8,128)} %fusion.50.extra_ref.proj_ref, ...), custom_call_target="tpu_custom_call", output_to_operand_aliasing={{0}: (20, {})} | custom-call | flops 98304000000 | bytes 14336000 | tf_op jit(solution)/shard_map/mixer_backward/pallas_call | solution.py:494
  301.3 4.7 %collective-permute-done.50 = bf16[128,2048]{1,0:T(8,128)(2,1)S(1)} collective-permute-done((bf16[128,2048]{1,0:T(8,128)(2,1)S(1)}, bf16[128,2048]{1,0:T(8,128)(2,1)S(1)}, u32[]{:S(2)}, u32[]{:S(2)}) %collective-permute-start.50) | collective-permute-done | bytes 524320 | tf_op jit(solution)/shard_map/ppermute | solution.py:684
  307.6 8.4 %convolution_convert_fusion.3 = bf16[1024,1024]{1,0:T(8,128)(2,1)} fusion(bf16[1024,1664]{1,0:T(8,128)(2,1)} %get-tuple-element.227, bf16[1024,1664]{1,0:T(8,128)(2,1)} %all-gather.2.cloned.1.call-done), kind=kOutput, calls=%fused_computation.11 | convolution fusion | flops 3490709504 | bytes 8912896 | tf_op jit(solution)/shard_map/dot_general | solution.py:676
  316.1 5.6 %convolution_convert_fusion.1 = bf16[512,1536]{1,0:T(8,128)(2,1)} fusion(bf16[1024,1664]{1,0:T(8,128)(2,1)} %get-tuple-element.227, pred[]{:T(512)S(6)} %eq.69, bf16[1024,128]{1,0:T(8,128)(2,1)S(1)} %copy-done.53, bf16[1024,128]{1,0:T(8,128)(2,1)} %get-tuple-element.293, bf16[1024,128]{1,0:T(8,128)(2,1)} %get-tuple-element.294, ...), kind=kOutput, calls=%fused_computation.4 | convolution fusion | flops 1620312064 | bytes 6815745 | tf_op jit(solution)/shard_map/dot_general | solution.py:676
  336.5 6.7 %collective-permute-done.59 = bf16[128,1536]{1,0:T(8,128)(2,1)S(1)} collective-permute-done((bf16[128,1536]{1,0:T(8,128)(2,1)S(1)}, bf16[128,1536]{1,0:T(8,128)(2,1)S(1)}, u32[]{:S(2)}, u32[]{:S(2)}) %collective-permute-start.59) | collective-permute-done | bytes 393248 | tf_op jit(solution)/shard_map/ppermute | solution.py:684
  343.1 9.2 %collective-permute-done.60 = bf16[128,1536]{1,0:T(8,128)(2,1)S(1)} collective-permute-done((bf16[128,1536]{1,0:T(8,128)(2,1)S(1)}, bf16[128,1536]{1,0:T(8,128)(2,1)S(1)}, u32[]{:S(2)}, u32[]{:S(2)}) %collective-permute-start.60) | collective-permute-done | bytes 393248 | tf_op jit(solution)/shard_map/ppermute | solution.py:684
  373.7 7.9 %collective-permute-done.63 = bf16[128,512]{1,0:T(8,128)(2,1)S(1)} collective-permute-done((bf16[128,512]{1,0:T(8,128)(2,1)S(1)}, bf16[128,512]{1,0:T(8,128)(2,1)S(1)}, u32[]{:S(2)}, u32[]{:S(2)}) %collective-permute-start.63) | collective-permute-done | bytes 131104 | tf_op jit(solution)/shard_map/ppermute | solution.py:750
  (443 shorter events, 155.0 us)
Async XLA Ops:
  7.2 50.9 %all-gather.2.cloned.1.call-start = ((), (), s32[]{:S(2)}) async-start(), calls=%async_computation.1 | async-start | bytes 3833856 | tf_op jit(solution)/shard_map/all_gather | solution.py:1036
  11.8 372.0 %reduce-scatter.2.cloned.1.call-start = ((), (), s32[]{:S(2)}) async-start(), calls=%async_computation.2 | async-start | bytes 2621440 | tf_op jit(solution)/shard_map/reduce_scatter | solution.py:1146
  20.2 23.7 %collective-permute-start.6 = (bf16[128,512]{0,1:T(8,128)(2,1)S(1)}, bf16[128,512]{0,1:T(8,128)(2,1)S(1)}, u32[]{:S(2)}, u32[]{:S(2)}) collective-permute-start(bf16[128,512]{0,1:T(8,128)(2,1)S(1)} %bitcast.124), channel_id=1, source_target_pairs={{0,3},{1,0},{2,1},{3,2},{4,7},{5,4},{6,5},{7,6},{8,11},{9,8},{10,9... | collective-permute-start | bytes 393224 | tf_op jit(solution)/shard_map/ppermute | solution.py:750
  24.9 22.9 %collective-permute-start.7 = (bf16[128,512]{0,1:T(8,128)(2,1)S(1)}, bf16[128,512]{0,1:T(8,128)(2,1)S(1)}, u32[]{:S(2)}, u32[]{:S(2)}) collective-permute-start(bf16[128,512]{0,1:T(8,128)(2,1)S(1)} %bitcast.125), channel_id=1, source_target_pairs={{0,2},{1,3},{2,0},{3,1},{4,6},{5,7},{6,4},{7,5},{8,10},{9,11},{10,... | collective-permute-start | bytes 393224 | tf_op jit(solution)/shard_map/ppermute | solution.py:750
  24.9 22.9 %collective-permute-start.8 = (bf16[128,512]{0,1:T(8,128)(2,1)S(1)}, bf16[128,512]{0,1:T(8,128)(2,1)}, u32[]{:S(2)}, u32[]{:S(2)}) collective-permute-start(bf16[128,512]{0,1:T(8,128)(2,1)S(1)} %bitcast.126), channel_id=1, source_target_pairs={{0,1},{1,2},{2,3},{3,0},{4,5},{5,6},{6,7},{7,4},{8,9},{9,10},{10,1... | collective-permute-start | bytes 393224 | tf_op jit(solution)/shard_map/ppermute | solution.py:750
  74.8 27.3 %collective-permute-start.9 = (bf16[3,704,128]{2,1,0:T(8,128)(2,1)S(1)}, bf16[3,704,128]{2,1,0:T(8,128)(2,1)S(1)}, u32[]{:S(2)}, u32[]{:S(2)}) collective-permute-start(bf16[3,704,128]{2,1,0:T(8,128)(2,1)S(1)} %pad_maximum_fusion.9), channel_id=1, source_target_pairs={{1,0},{0,2},{2,3},{3,1},{5,4},{4,6},{6,7},{7,5},{9,8},{8,10},{10,1... | collective-permute-start | bytes 1622024 | tf_op jit(solution)/shard_map/ppermute | solution.py:913
  76.1 26.0 %collective-permute-start.10 = (bf16[3,704,128]{2,1,0:T(8,128)(2,1)S(1)}, bf16[3,704,128]{2,1,0:T(8,128)(2,1)S(1)}, u32[]{:S(2)}, u32[]{:S(2)}) collective-permute-start(bf16[3,704,128]{2,1,0:T(8,128)(2,1)S(1)} %pad_maximum_fusion.9), channel_id=1, source_target_pairs={{2,1},{1,2},{6,5},{5,6},{10,9},{9,10},{14,13},{13,14},{18,17},{17,... | collective-permute-start | bytes 1622024 | tf_op jit(solution)/shard_map/ppermute | solution.py:914
  77.4 24.8 %collective-permute-start.11 = (bf16[128,2048]{0,1:T(8,128)(2,1)S(1)}, bf16[128,2048]{0,1:T(8,128)(2,1)S(1)}, u32[]{:S(2)}, u32[]{:S(2)}) collective-permute-start(bf16[128,2048]{0,1:T(8,128)(2,1)S(1)} %pad_maximum_fusion.10), channel_id=1, source_target_pairs={{0,8},{4,12},{8,0},{12,4},{16,24},{20,28},{24,16},{28,20},{1,9},{5... | collective-permute-start | bytes 1572872 | tf_op jit(solution)/shard_map/ppermute | solution.py:684
  78.9 23.2 %collective-permute-start.12 = (bf16[128,2048]{0,1:T(8,128)(2,1)S(1)}, bf16[128,2048]{0,1:T(8,128)(2,1)S(1)}, u32[]{:S(2)}, u32[]{:S(2)}) collective-permute-start(bf16[128,2048]{0,1:T(8,128)(2,1)S(1)} %pad_maximum_fusion.10), channel_id=1, source_target_pairs={{0,16},{4,20},{8,24},{12,28},{16,0},{20,4},{24,8},{28,12},{1,17},{... | collective-permute-start | bytes 1572872 | tf_op jit(solution)/shard_map/ppermute | solution.py:684
  104.0 50.1 %collective-permute-start.21 = (bf16[128,2048]{0,1:T(8,128)(2,1)S(1)}, bf16[128,2048]{0,1:T(8,128)(2,1)S(1)}, u32[]{:S(2)}, u32[]{:S(2)}) collective-permute-start(bf16[128,2048]{0,1:T(8,128)(2,1)S(1)} %pad_maximum_fusion.10), channel_id=1, source_target_pairs={{0,4},{4,0},{8,12},{12,8},{16,20},{20,16},{24,28},{28,24},{1,5},{5... | collective-permute-start | bytes 1572872 | tf_op jit(solution)/shard_map/ppermute | solution.py:684
  106.6 52.2 %collective-permute-start.28 = (bf16[256,1024]{1,0:T(8,128)(2,1)S(1)}, bf16[256,1024]{1,0:T(8,128)(2,1)}, u32[]{:S(2)}, u32[]{:S(2)}) collective-permute-start(bf16[256,1024]{1,0:T(8,128)(2,1)S(1)} %copy-done.29), channel_id=1, source_target_pairs={{0,4},{4,0},{8,12},{12,8},{16,20},{20,16},{24,28},{28,24},{1,5},{5... | collective-permute-start | bytes 1572872 | tf_op jit(solution)/shard_map/ppermute | solution.py:684
  127.9 23.8 %collective-permute-start.19 = (bf16[256,512]{1,0:T(8,128)(2,1)S(1)}, bf16[256,512]{1,0:T(8,128)(2,1)S(1)}, u32[]{:S(2)}, u32[]{:S(2)}) collective-permute-start(bf16[256,512]{1,0:T(8,128)(2,1)S(1)} %get-tuple-element.330), channel_id=1, source_target_pairs={{0,2},{1,3},{2,0},{3,1},{4,6},{5,7},{6,4},{7,5},{8,10},{9,11},{10,... | collective-permute-start | bytes 786440 | tf_op jit(solution)/shard_map/ppermute | solution.py:750
  128.9 22.8 %collective-permute-start.20 = (bf16[256,512]{1,0:T(8,128)(2,1)S(1)}, bf16[256,512]{1,0:T(8,128)(2,1)S(1)}, u32[]{:S(2)}, u32[]{:S(2)}) collective-permute-start(bf16[256,512]{1,0:T(8,128)(2,1)S(1)} %get-tuple-element.329), channel_id=1, source_target_pairs={{0,1},{1,2},{2,3},{3,0},{4,5},{5,6},{6,7},{7,4},{8,9},{9,10},{10,1... | collective-permute-start | bytes 786440 | tf_op jit(solution)/shard_map/ppermute | solution.py:750
  134.7 40.2 %collective-permute-start.30 = (bf16[2,3,704,128]{3,2,1,0:T(8,128)(2,1)}, bf16[2,3,704,128]{3,2,1,0:T(8,128)(2,1)}, u32[]{:S(2)}, u32[]{:S(2)}) collective-permute-start(bf16[2,3,704,128]{3,2,1,0:T(8,128)(2,1)} %pad_maximum_fusion.2.refs_0_), channel_id=1, source_target_pairs={{0,16},{4,20},{8,24},{12,28},{16,0},{20,4},{24,8},{28,12},{1,17},{... | collective-permute-start | bytes 3244040 | tf_op jit(solution)/shard_map/ppermute | solution.py:684
  154.5 26.6 %collective-permute-start.31 = (bf16[2,3,704,128]{3,2,1,0:T(8,128)(2,1)}, bf16[2,3,704,128]{3,2,1,0:T(8,128)(2,1)}, u32[]{:S(2)}, u32[]{:S(2)}) collective-permute-start(bf16[2,3,704,128]{3,2,1,0:T(8,128)(2,1)} %pad_maximum_fusion.3.refs_2_), channel_id=1, source_target_pairs={{0,8},{4,12},{8,0},{12,4},{16,24},{20,28},{24,16},{28,20},{1,9},{5... | collective-permute-start | bytes 3244040 | tf_op jit(solution)/shard_map/ppermute | solution.py:684
  221.5 25.6 %collective-permute-start.38 = (bf16[2,3,704,128]{3,2,1,0:T(8,128)(2,1)S(1)}, bf16[2,3,704,128]{3,2,1,0:T(8,128)(2,1)S(1)}, u32[]{:S(2)}, u32[]{:S(2)}) collective-permute-start(bf16[2,3,704,128]{3,2,1,0:T(8,128)(2,1)S(1)} %pad_maximum_fusion.4), channel_id=1, source_target_pairs={{0,8},{4,12},{8,0},{12,4},{16,24},{20,28},{24,16},{28,20},{1,9},{5... | collective-permute-start | bytes 3244040 | tf_op jit(solution)/shard_map/ppermute | solution.py:684
  222.2 25.3 %collective-permute-start.39 = (bf16[2,3,704,128]{3,2,1,0:T(8,128)(2,1)S(1)}, bf16[2,3,704,128]{3,2,1,0:T(8,128)(2,1)S(1)}, u32[]{:S(2)}, u32[]{:S(2)}) collective-permute-start(bf16[2,3,704,128]{3,2,1,0:T(8,128)(2,1)S(1)} %slice.240), channel_id=1, source_target_pairs={{0,16},{4,20},{8,24},{12,28},{16,0},{20,4},{24,8},{28,12},{1,17},{... | collective-permute-start | bytes 3244040 | tf_op jit(solution)/shard_map/ppermute | solution.py:684
  227.8 25.3 %collective-permute-start.35 = (bf16[256,512]{1,0:T(8,128)(2,1)S(1)}, bf16[256,512]{1,0:T(8,128)(2,1)S(1)}, u32[]{:S(2)}, u32[]{:S(2)}) collective-permute-start(bf16[256,512]{1,0:T(8,128)(2,1)S(1)} %get-tuple-element.327), channel_id=1, source_target_pairs={{0,1},{1,2},{2,3},{3,0},{4,5},{5,6},{6,7},{7,4},{8,9},{9,10},{10,1... | collective-permute-start | bytes 786440 | tf_op jit(solution)/shard_map/ppermute | solution.py:750
  228.1 24.9 %collective-permute-start.36 = (bf16[256,512]{1,0:T(8,128)(2,1)S(1)}, bf16[256,512]{1,0:T(8,128)(2,1)S(1)}, u32[]{:S(2)}, u32[]{:S(2)}) collective-permute-start(bf16[256,512]{1,0:T(8,128)(2,1)S(1)} %get-tuple-element.326), channel_id=1, source_target_pairs={{0,2},{1,3},{2,0},{3,1},{4,6},{5,7},{6,4},{7,5},{8,10},{9,11},{10,... | collective-permute-start | bytes 786440 | tf_op jit(solution)/shard_map/ppermute | solution.py:750
  229.9 23.2 %collective-permute-start.37 = (bf16[256,512]{1,0:T(8,128)(2,1)S(1)}, bf16[256,512]{1,0:T(8,128)(2,1)S(1)}, u32[]{:S(2)}, u32[]{:S(2)}) collective-permute-start(bf16[256,512]{1,0:T(8,128)(2,1)S(1)} %get-tuple-element.325), channel_id=1, source_target_pairs={{0,3},{1,0},{2,1},{3,2},{4,7},{5,4},{6,5},{7,6},{8,11},{9,8},{10,9... | collective-permute-start | bytes 786440 | tf_op jit(solution)/shard_map/ppermute | solution.py:750
  251.4 23.9 %collective-permute-start.45 = (bf16[512,2048]{1,0:T(8,128)(2,1)}, bf16[512,2048]{1,0:T(8,128)(2,1)}, u32[]{:S(2)}, u32[]{:S(2)}) collective-permute-start(bf16[512,2048]{1,0:T(8,128)(2,1)} %convolution_convert_fusion), channel_id=1, source_target_pairs={{0,4},{4,0},{8,12},{12,8},{16,20},{20,16},{24,28},{28,24},{1,5},{5... | collective-permute-start | bytes 6291464 | tf_op jit(solution)/shard_map/ppermute | solution.py:684
  253.1 22.3 %collective-permute-start.42 = (bf16[256,1024]{1,0:T(8,128)(2,1)}, bf16[256,1024]{1,0:T(8,128)(2,1)}, u32[]{:S(2)}, u32[]{:S(2)}) collective-permute-start(bf16[256,1024]{1,0:T(8,128)(2,1)} %get-tuple-element.205), channel_id=1, source_target_pairs={{0,1},{1,0},{2,3},{3,2},{4,5},{5,4},{6,7},{7,6},{8,9},{9,8},{10,11... | collective-permute-start | bytes 1572872 | tf_op jit(solution)/shard_map/ppermute | solution.py:684
  280.7 25.3 %collective-permute-start.50 = (bf16[128,2048]{1,0:T(8,128)(2,1)S(1)}, bf16[128,2048]{1,0:T(8,128)(2,1)S(1)}, u32[]{:S(2)}, u32[]{:S(2)}) collective-permute-start(bf16[128,2048]{1,0:T(8,128)(2,1)S(1)} %get-tuple-element.300), channel_id=1, source_target_pairs={{0,16},{4,20},{8,24},{12,28},{16,0},{20,4},{24,8},{28,12},{1,17},{... | collective-permute-start | bytes 1572872 | tf_op jit(solution)/shard_map/ppermute | solution.py:684
  281.2 24.8 %collective-permute-start.51 = (bf16[128,2048]{1,0:T(8,128)(2,1)S(1)}, bf16[128,2048]{1,0:T(8,128)(2,1)S(1)}, u32[]{:S(2)}, u32[]{:S(2)}) collective-permute-start(bf16[128,2048]{1,0:T(8,128)(2,1)S(1)} %get-tuple-element.299), channel_id=1, source_target_pairs={{0,24},{4,28},{8,16},{12,20},{16,8},{20,12},{24,0},{28,4},{1,25},{... | collective-permute-start | bytes 1572872 | tf_op jit(solution)/shard_map/ppermute | solution.py:684
  (136 other events, 1396.5 us)
Sparse Core Ops, SparseCore 0:
  11.9 36.1 all-gather.1
  325.2 47.5 reduce-scatter.1
where the time goes:
time: 399 us; the launch traced here: 395 us
  waiting for transfers between devices  107 us (27%)
  Pallas kernels  85.4 us (21%)
  starting transfers between devices  82.3 us (21%)
  local copies, waits for them, and re-layouts  40.3 us (10%)
  matrix products  32.7 us (8%)
  other arithmetic  30.9 us (8%)
  between operations  15.9 us (4%)
    ppermute x40, waiting for transfers between devices, exchange(): lax.ppermute(x, axis, [(i, i ^ bit) for i in range(lax.axis_size(axis))])  62.9 us
    dot_general x9, matrix products, product(): lax.dot_general(left, right, (dims, ((), ())), preferred_element_type=f32)  32.7 us
    pallas_call x2, Pallas kernels, mixer_backward(): pl.pallas_call(functools.partial(backward_body, heads, prec), grid=(steps...  31.2 us
    ppermute x15, waiting for transfers between devices, shifted(): return lax.ppermute(x, axis, [(i, (i + by) % ways) for i in range(ways)])  29.2 us
    pallas_call x2, Pallas kernels, mixer_forward(): pl.pallas_call(functools.partial(forward_body, heads, prec), grid=(steps,...  27.8 us
    ppermute x15, starting transfers between devices, shifted(): return lax.ppermute(x, axis, [(i, (i + by) % ways) for i in range(ways)])  27.1 us
    ppermute x40, starting transfers between devices, exchange(): lax.ppermute(x, axis, [(i, i ^ bit) for i in range(lax.axis_size(axis))])  26.2 us
    ppermute x3, starting transfers between devices, line_gather(): below.append(lax.ppermute(below[-1], axis, up))  21.5 us
  transfers between devices with their start and end apart: 67, of which 21 were waited for; matrix products, arithmetic and copies ran while one was open for 16% of the time, Pallas kernels for 18%

commit v1 on v0

--- a/solution.py
+++ b/solution.py
@@ -539,9 +539,24 @@
     return jnp.pad(head, ((0, 6), (BETA_AT + heads, LANES - BETA_AT - 2 * heads)))
 
 
-def ffn_body(where, place_ref, rows_ref, cot_ref, *refs):
-    w_refs = refs[:-5]
-    gate_ref, up_ref, hidden_ref, back_ref, out_ref = refs[-5:]
+def ffn_body(where, runs, place_ref, *refs):
+    step = pl.program_id(0)
+    each = pl.num_programs(0) // runs
+    rows_refs = refs[:runs]
+    cot_refs = refs[runs : 2 * runs]
+    outs = refs[len(refs) - 2 * runs - 5 :]
+    w_refs = refs[2 * runs : len(refs) - 2 * runs - 5]
+    gate_ref, up_ref, hidden_ref = outs[:3]
+    back_refs = outs[3 : 3 + runs]
+    out_refs = outs[3 + runs : 3 + 2 * runs]
+    rows_ref, cot_ref = outs[3 + 2 * runs :]
+    for i in range(runs):
+
+        @pl.when(step // each == i)
+        def _():
+            rows_ref[...] = rows_refs[i][...]
+            cot_ref[...] = cot_refs[i][...]
+
     pieces = len(where[0])
     size = rows_ref.shape[1] // pieces
 
@@ -581,43 +596,63 @@
         back = back + lax.dot_general(
             grad_up, weight(p, 1), (NN, ((), ())), preferred_element_type=f32
         )
-        back_ref[:, own] = back.astype(bf16)
-        out_ref[:, own] = lax.dot_general(
+        rows_ref[:, own] = back.astype(bf16)
+        cot_ref[:, own] = lax.dot_general(
             hidden, weight(p, 2), (NN, ((), ())), preferred_element_type=f32
         ).astype(bf16)
+    for i in range(runs):
+
+        @pl.when(step // each == i)
+        def _():
+            back_refs[i][...] = rows_ref[...]
+            out_refs[i][...] = cot_ref[...]
 
 
 FFN_TILE = 256
 
 
 def ffn_both(place, rows, cot, weights, where):
-    count, d = rows.shape
+    runs = len(rows)
+    count, d = rows[0].shape
+    each = count // FFN_TILE
+    total = runs * count
     hidden = weights[0].shape[2]
-    tile = lambda width: pl.BlockSpec((FFN_TILE, width), lambda c, place: (c, 0))
+
+    def run_tile(i):
+        return pl.BlockSpec(
+            (FFN_TILE, d), lambda c, place: (jnp.clip(c - i * each, 0, each - 1), 0)
+        )
+
+    tiles = [run_tile(i) for i in range(runs)]
+    wide = pl.BlockSpec((FFN_TILE, hidden), lambda c, place: (c, 0))
     full = pl.BlockSpec(weights[0].shape, lambda c, place: (0, 0, 0, 0))
-    return pl.pallas_call(
-        functools.partial(ffn_body, where),
+    gate, up, hidden_out, *out = pl.pallas_call(
+        functools.partial(ffn_body, where, runs),
         grid_spec=pltpu.PrefetchScalarGridSpec(
             num_scalar_prefetch=1,
-            grid=(count // FFN_TILE,),
-            in_specs=[tile(d), tile(d)] + [full] * len(weights),
-            out_specs=[tile(hidden), tile(hidden), tile(hidden), tile(d), tile(d)],
+            grid=(runs * each,),
+            in_specs=tiles + tiles + [full] * len(weights),
+            out_specs=[wide] * 3 + tiles + tiles,
+            scratch_shapes=[pltpu.VMEM((FFN_TILE, d), bf16)] * 2,
         ),
-        out_shape=[
-            jax.ShapeDtypeStruct((count, width), bf16) for width in (hidden, hidden, hidden, d, d)
-        ],
+        out_shape=[jax.ShapeDtypeStruct((total, hidden), bf16)] * 3
+        + [jax.ShapeDtypeStruct((count, d), bf16)] * (2 * runs),
         compiler_params=pltpu.CompilerParams(
             dimension_semantics=("arbitrary",), vmem_limit_bytes=BUDGET
         ),
         cost_estimate=pl.CostEstimate(
-            flops=24 * count * d * hidden, bytes_accessed=8 * count * d, transcendentals=0
+            flops=24 * total * d * hidden, bytes_accessed=8 * total * d, transcendentals=0
         ),
         name="ffn_both",
-    )(place.reshape(1), rows, cot, *weights)
-
-
-def ffn_grads_body(place_ref, rows_ref, cot_ref, gate_ref, up_ref, hidden_ref, *refs):
-    out_refs = refs[:-1]
+    )(place.reshape(1), *rows, *cot, *weights)
+    return gate, up, hidden_out, out[:runs], out[runs:]
+
+
+def ffn_grads_body(runs, place_ref, *refs):
+    rows_refs = refs[:runs]
+    cot_refs = refs[runs : 2 * runs]
+    gate_ref, up_ref, hidden_ref = refs[2 * runs : 2 * runs + 3]
+    out_refs = refs[2 * runs + 3 : -1]
     flipped_ref = refs[-1]
 
     @pl.when(pl.program_id(0) == 0)
@@ -625,41 +660,45 @@
         for i, ref in enumerate((gate_ref, up_ref, hidden_ref)):
             flipped_ref[i] = ref[...].T
 
-    lanes = rows_ref.shape[1] // len(out_refs)
-    for i, right in enumerate((rows_ref, rows_ref, cot_ref)):
+    rows = jnp.concatenate([ref[...] for ref in rows_refs], 0)
+    cot = jnp.concatenate([ref[...] for ref in cot_refs], 0)
+    lanes = rows.shape[1] // len(out_refs)
+    for i, right in enumerate((rows, rows, cot)):
         grad = lax.dot_general(
-            flipped_ref[i], right[...], (NN, ((), ())), preferred_element_type=f32
+            flipped_ref[i], right, (NN, ((), ())), preferred_element_type=f32
         ).astype(bf16)
         for j, out_ref in enumerate(out_refs):
             out_ref[0, i] = grad[:, j * lanes : (j + 1) * lanes]
 
 
 def ffn_weight_grads(place, rows, cot, gate, up, hidden, pieces, split):
-    count, d = rows.shape
+    runs = len(rows)
+    count, d = rows[0].shape
+    total = runs * count
     width = hidden.shape[1]
     size = d // pieces
     column = pl.BlockSpec((count, size), lambda p, place: (0, p ^ place[0]))
-    full = pl.BlockSpec((count, width), lambda p, place: (0, 0))
+    full = pl.BlockSpec((total, width), lambda p, place: (0, 0))
     return pl.pallas_call(
-        ffn_grads_body,
+        functools.partial(ffn_grads_body, runs),
         grid_spec=pltpu.PrefetchScalarGridSpec(
             num_scalar_prefetch=1,
             grid=(pieces,),
-            in_specs=[column, column, full, full, full],
+            in_specs=[column] * (2 * runs) + [full] * 3,
             out_specs=[
                 pl.BlockSpec((1, 3, width, size // split), lambda p, place: (p, 0, 0, 0))
             ] * split,
-            scratch_shapes=[pltpu.VMEM((3, width, count), bf16)],
+            scratch_shapes=[pltpu.VMEM((3, width, total), bf16)],
         ),
         out_shape=[jax.ShapeDtypeStruct((pieces, 3, width, size // split), bf16)] * split,
         compiler_params=pltpu.CompilerParams(
             dimension_semantics=("arbitrary",), vmem_limit_bytes=BUDGET
         ),
         cost_estimate=pl.CostEstimate(
-            flops=12 * count * d * width, bytes_accessed=8 * count * d, transcendentals=0
+            flops=12 * total * d * width, bytes_accessed=8 * total * d, transcendentals=0
         ),
         name="ffn_weight_grads",
-    )(place.reshape(1), rows, cot, gate, up, hidden)
+    )(place.reshape(1), *rows, *cot, gate, up, hidden)
 
 
 def norm_factor(values):
@@ -869,11 +908,14 @@
     def reach(self, x):
         return line_gather(x, "tensor")[0]
 
-    def gather(self, x, far):
-        return far
+    def beside(self, x):
+        return ()
+
+    def gather(self, x, near, far):
+        return [far]
 
     def halves(self, x):
-        return line_scatter(x, "tensor")[0], jnp.zeros((), bf16)
+        return line_scatter(x[0], "tensor")[0], jnp.zeros((), bf16)
 
     def cross(self, far):
         return far
@@ -944,14 +986,15 @@
     def reach(self, x):
         return exchange(x, "tensor", 1)
 
-    def gather(self, x, far):
-        return jnp.concatenate([x, exchange(x, "dp", 1), far, exchange(far, "dp", 1)], 0)
+    def beside(self, x):
+        return exchange(x, "dp", 1)
+
+    def gather(self, x, near, far):
+        return [x, near, far, exchange(far, "dp", 1)]
 
     def halves(self, x):
-        size = x.shape[0] // 4
-        parts = [x[i * size : (i + 1) * size] for i in range(4)]
-        far = (parts[2].astype(f32) + exchange(parts[3], "dp", 1).astype(f32)).astype(bf16)
-        return parts[0].astype(f32) + exchange(parts[1], "dp", 1).astype(f32), far
+        far = (x[2].astype(f32) + exchange(x[3], "dp", 1).astype(f32)).astype(bf16)
+        return x[0].astype(f32) + exchange(x[1], "dp", 1).astype(f32), far
 
     def cross(self, far):
         return exchange(far, "tensor", 1)
@@ -1063,11 +1106,16 @@
     onorm_row = w_onorm.astype(f32).reshape(1, heads * DV)
     head_rows = head_lanes(head_local)
     places = token_places(segments)
-    rows_one, (out_weights.rows, constants, places) = line_gather(
-        normed_one, "tensor", (out_weights.rows, (conv_rows, head_rows, onorm_row), places)
+    kind = PairFfn if teams == 4 and ways == 8 else LineFfn
+    rows_one, (out_weights.rows, constants, places, cot_near) = line_gather(
+        normed_one,
+        "tensor",
+        (
+            out_weights.rows, (conv_rows, head_rows, onorm_row), places,
+            kind.beside(None, cotangent),
+        ),
     )
     out_weights.start(rows_one)
-    kind = PairFfn if teams == 4 and ways == 8 else LineFfn
     ffn = kind(ffn_in, ffn_out, rows_one)
     wide = heads * MIX
     proj = product(rows_one, w_in, NN)
@@ -1085,13 +1133,13 @@
     ffn.plane_step()
     came = swap_parts(lambda i: lax.dynamic_slice_in_dim(mixed, i * own, own, 0), "tensor")
     out_t = out_weights.finish(came[-1])
-    grad_rows = ffn.gather(cotangent, after(cot_far, came[-1]))
+    grad_rows = ffn.gather(cotangent, cot_near, after(cot_far, came[-1]))
     mixed = jnp.concatenate(ordered(came, "tensor"), 1)
     middle = inputs + product(mixed, out_t, NT)
     factor_two = norm_factor(middle)
     scaled_two = middle * factor_two
     normed_two = (scaled_two * gains[1]).astype(bf16)
-    rows_two = ffn.gather(normed_two, ffn.reach(normed_two))
+    rows_two = ffn.gather(normed_two, ffn.beside(normed_two), ffn.reach(normed_two))
     w_ffn = ffn.finish(normed_two)
     grad_gate, grad_up, hidden, back, forth = ffn_both(
         ffn.place, rows_two, grad_rows, w_ffn, ffn.where
@@ -1169,9 +1217,7 @@
     totals = sum_over(jnp.concatenate(parts), "dp")
     shared = totals[: sizes[0]]
     shared = sum(ordered(swap_parts(lambda i: shared, "tensor"), "tensor"))
-    grad_in.parts, out_parts = lax.optimization_barrier(
-        (grad_in.parts, out_sum.finish().astype(bf16))
-    )
+    out_parts = after(out_sum.finish().astype(bf16), grad_in.total)
     out_out = sum(block.astype(f32) for block in out_weights.send_sum(out_parts, width))
     conv_total, onorm_total, small_total = (totals[ends[i] : ends[i + 1]] for i in (1, 2, 3))
     place = lax.axis_index("dp")

time: 399 us -> 391 us (0.980)
  waiting for transfers between devices: 107 us -> 101 us
  local copies, waits for them, and re-layouts: 40.3 us -> 35.6 us
    ppermute x40, waiting for transfers between devices: 62.9 us -> 56 us  [exchange(): lax.ppermute(x, axis, [(i, i ^ bit) for i in range(lax.axis_size(axis))])]
    unnamed x193 -> x202, local copies, waits for them, and re-layouts: 10.6 us -> 8.34 us
  transfers between devices with their start and end apart: 67 -> 67, of which waited for: 21 -> 20; matrix products, arithmetic and copies ran while one was open for 16% -> 16% of each run, Pallas kernels for 18% -> 18%
where the time goes in v1:
time: 391 us; the launch traced here: 387 us
  waiting for transfers between devices  101 us (26%)
  Pallas kernels  88.8 us (23%)
  starting transfers between devices  84.8 us (22%)
  local copies, waits for them, and re-layouts  35.6 us (9%)
  matrix products  32.6 us (8%)
  other arithmetic  28.2 us (7%)
  between operations  16 us (4%)
    ppermute x40, waiting for transfers between devices, exchange(): lax.ppermute(x, axis, [(i, i ^ bit) for i in range(lax.axis_size(axis))])  56 us
    dot_general x9, matrix products, product(): lax.dot_general(left, right, (dims, ((), ())), preferred_element_type=f32)  32.6 us
    pallas_call x2, Pallas kernels, mixer_backward(): pl.pallas_call(functools.partial(backward_body, heads, prec), grid=(steps...  31.2 us
    ppermute x15, waiting for transfers between devices, shifted(): return lax.ppermute(x, axis, [(i, (i + by) % ways) for i in range(ways)])  30.8 us
    ppermute x40, starting transfers between devices, exchange(): lax.ppermute(x, axis, [(i, i ^ bit) for i in range(lax.axis_size(axis))])  28.2 us
    pallas_call x2, Pallas kernels, mixer_forward(): pl.pallas_call(functools.partial(forward_body, heads, prec), grid=(steps,...  27.8 us
    ppermute x15, starting transfers between devices, shifted(): return lax.ppermute(x, axis, [(i, (i + by) % ways) for i in range(ways)])  27.4 us
    ppermute x3, starting transfers between devices, line_gather(): below.append(lax.ppermute(below[-1], axis, up))  21.6 us
  transfers between devices with their start and end apart: 67, of which 20 were waited for; matrix products, arithmetic and copies ran while one was open for 16% of the time, Pallas kernels for 18%

profile of v1, /device:TPU:0, one launch (start us, length us, event | category | flops | bytes accessed | tf_op | source)
XLA Modules:
  0.0 387.1 jit_solution(12175538911383949953)
XLA Ops:
  14.0 5.1 %collective-permute-start = (bf16[256,1024]{1,0:T(8,128)(2,1)S(1)}, bf16[256,1024]{1,0:T(8,128)(2,1)S(1)}, u32[]{:S(2)}, u32[]{:S(2)}) collective-permute-start(bf16[256,1024]{1,0:T(8,128)(2,1)S(1)} %fusion.10), channel_id=1, source_target_pairs={{0,1},{1,2},{2,3},{4,5},{5,6},{6,7},{8,9},{9,10},{10,11},{12,13},{... | collective-permute-start | bytes 1572872 | tf_op jit(solution)/shard_map/ppermute | solution.py:745
  20.4 5.4 %collective-permute-start.6 = (bf16[128,512]{0,1:T(8,128)(2,1)S(1)}, bf16[128,512]{0,1:T(8,128)(2,1)}, u32[]{:S(2)}, u32[]{:S(2)}) collective-permute-start(bf16[128,512]{0,1:T(8,128)(2,1)S(1)} %bitcast.124), channel_id=1, source_target_pairs={{0,3},{1,0},{2,1},{3,2},{4,7},{5,4},{6,5},{7,6},{8,11},{9,8},{10,9... | collective-permute-start | bytes 393224 | tf_op jit(solution)/shard_map/ppermute | solution.py:789
  27.1 4.2 %collective-permute-done = bf16[256,1024]{1,0:T(8,128)(2,1)S(1)} collective-permute-done((bf16[256,1024]{1,0:T(8,128)(2,1)S(1)}, bf16[256,1024]{1,0:T(8,128)(2,1)S(1)}, u32[]{:S(2)}, u32[]{:S(2)}) %collective-permute-start) | collective-permute-done | bytes 524320 | tf_op jit(solution)/shard_map/ppermute | solution.py:745
  31.3 9.5 %collective-permute-start.1 = (bf16[256,1024]{1,0:T(8,128)(2,1)S(1)}, bf16[256,1024]{1,0:T(8,128)(2,1)}, u32[]{:S(2)}, u32[]{:S(2)}) collective-permute-start(bf16[256,1024]{1,0:T(8,128)(2,1)S(1)} %collective-permute-done), channel_id=1, source_target_pairs={{0,1},{1,2},{2,3},{4,5},{5,6},{6,7},{8,9},{9,10},{10,11},{12,13},{... | collective-permute-start | bytes 1572872 | tf_op jit(solution)/shard_map/ppermute | solution.py:745
  49.9 7.0 %collective-permute-start.2 = (bf16[256,1024]{1,0:T(8,128)(2,1)}, bf16[256,1024]{1,0:T(8,128)(2,1)}, u32[]{:S(2)}, u32[]{:S(2)}) collective-permute-start(bf16[256,1024]{1,0:T(8,128)(2,1)} %collective-permute-done.1), channel_id=1, source_target_pairs={{0,1},{1,2},{2,3},{4,5},{5,6},{6,7},{8,9},{9,10},{10,11},{12,13},{... | collective-permute-start | bytes 1572872 | tf_op jit(solution)/shard_map/ppermute | solution.py:745
  62.3 4.4 %collective-permute-done.2 = bf16[256,1024]{1,0:T(8,128)(2,1)} collective-permute-done((bf16[256,1024]{1,0:T(8,128)(2,1)}, bf16[256,1024]{1,0:T(8,128)(2,1)}, u32[]{:S(2)}, u32[]{:S(2)}) %collective-permute-start.2) | collective-permute-done | bytes 524320 | tf_op jit(solution)/shard_map/ppermute | solution.py:745
  66.7 5.0 %collective-permute-done.5 = bf16[256,1024]{1,0:T(8,128)(2,1)} collective-permute-done((bf16[256,1024]{1,0:T(8,128)(2,1)}, bf16[256,1024]{1,0:T(8,128)(2,1)}, u32[]{:S(2)}, u32[]{:S(2)}) %collective-permute-start.5) | collective-permute-done | bytes 524320 | tf_op jit(solution)/shard_map/ppermute | solution.py:746
  81.2 5.9 %fusion.48.extra_ref.proj_ref = f32[1024,1664]{1,0:T(8,128)} fusion(bf16[1024,1024]{1,0:T(8,128)(2,1)S(1)} %pad_maximum_fusion, bf16[1024,1664]{1,0:T(8,128)(2,1)S(1)} %copy-done.76), kind=kOutput, calls=%fused_computation.170 | convolution fusion | flops 3489660928 | bytes 12320768 | tf_op jit(solution)/shard_map/dot_general | solution.py:715
  88.4 13.9 %mixer_forward.2 = (bf16[1024,512]{1,0:T(8,128)(2,1)}, f32[1024,1024]{1,0:T(8,128)}, f32[1024,512]{1,0:T(8,128)}, f32[1024,512]{1,0:T(8,128)}, f32[1024,256]{1,0...) custom-call(f32[1024,128]{1,0:T(8,128)} %pad.18.places_ref, ...), custom_call_target="tpu_custom_call" | custom-call | flops 65536000000 | bytes 12288000 | tf_op jit(solution)/shard_map/mixer_forward/pallas_call | solution.py:439
  109.4 13.9 %mixer_forward.3 = (bf16[1024,512]{1,0:T(8,128)(2,1)}, f32[1024,1024]{1,0:T(8,128)}, f32[1024,512]{1,0:T(8,128)}, f32[1024,512]{1,0:T(8,128)}, f32[1024,256]{1,0...) custom-call(f32[1024,128]{1,0:T(8,128)} %pad.18.places_ref, ...), custom_call_target="tpu_custom_call", output_to_operand_aliasing={{0}: (8, {}), {1}: (9, {}), {2}: (10, {}), {3}: (11, {}), {... | custom-call | flops 65536000000 | bytes 12288000 | tf_op jit(solution)/shard_map/mixer_forward/pallas_call | solution.py:439
  135.6 14.7 %collective-permute-done.20 = bf16[256,512]{1,0:T(8,128)(2,1)S(1)} collective-permute-done((bf16[256,512]{1,0:T(8,128)(2,1)S(1)}, bf16[256,512]{1,0:T(8,128)(2,1)S(1)}, u32[]{:S(2)}, u32[]{:S(2)}) %collective-permute-start.20) | collective-permute-done | bytes 262176 | tf_op jit(solution)/shard_map/ppermute | solution.py:789
  158.7 13.6 %collective-permute-done.27.refs_2_ = bf16[256,1024]{1,0:T(8,128)(2,1)} collective-permute-done((bf16[256,1024]{1,0:T(8,128)(2,1)}, bf16[256,1024]{1,0:T(8,128)(2,1)}, u32[]{:S(2)}, u32[]{:S(2)}) %collective-permute-start.27) | collective-permute-done | bytes 524320 | tf_op jit(solution)/shard_map/ppermute | solution.py:723
  174.5 18.8 %ffn_both.1 = (bf16[1024,704]{1,0:T(8,128)(2,1)}, bf16[1024,704]{1,0:T(8,128)(2,1)}, bf16[1024,704]{1,0:T(8,128)(2,1)}, bf16[256,1024]{1,0:T(8,128)(2,1)}, bf16[...) custom-call(s32[1]{0:T(128)} %bitcast.34.place_ref, ...), custom_call_target="tpu_custom_call" | custom-call | flops 17716740096 | bytes 8388608 | tf_op jit(solution)/shard_map/ffn_both/pallas_call | solution.py:629
  197.4 11.0 %ffn_weight_grads.1 = (bf16[4,3,704,128]{3,2,1,0:T(8,128)(2,1)}, bf16[4,3,704,128]{3,2,1,0:T(8,128)(2,1)}) custom-call(s32[1]{0:T(128)} %bitcast.34.place_ref, bf16[256,1024]{1,0:T(8,128)(2,1)} %multiply_convert_fusion.refs_0_, bf16[256,1024]{1,0:T(8,128)(2,1)} %collective-permute-done.26.refs_1_, bf16[256,1024]{1,0:T(8,128)(2,1)} %collective-permute-done.27.refs_2_, ...), custom_call_target="tpu_custom_call" | custom-call | flops 8858370048 | bytes 8388608 | tf_op jit(solution)/shard_map/ffn_weight_grads/pallas_call | solution.py:682
  224.2 13.5 %collective-permute-done.38 = bf16[2,3,704,128]{3,2,1,0:T(8,128)(2,1)S(1)} collective-permute-done((bf16[2,3,704,128]{3,2,1,0:T(8,128)(2,1)S(1)}, bf16[2,3,704,128]{3,2,1,0:T(8,128)(2,1)S(1)}, u32[]{:S(2)}, u32[]{:S(2)}) %collective-permute-start.38) | collective-permute-done | bytes 1081376 | tf_op jit(solution)/shard_map/ppermute | solution.py:723
  250.4 15.5 %mixer_backward.2 = (bf16[1024,1664]{1,0:T(8,128)(2,1)}, f32[2,128,256]{2,1,0:T(8,128)}, f32[8,1024]{1,0:T(8,128)}, f32[4,1024]{1,0:T(4,128)}, f32[8,128]{1,0:T(8,128)}, /*index=5*/f32[1,512]{1,0:T(1,128)}) custom-call(f32[1024,128]{1,0:T(8,128)} %pad.18.places_ref, f32[1024,1664]{1,0:T(8,128)} %fusion.48.extra_ref.proj_ref, ...), custom_call_target="tpu_custom_call" | custom-call | flops 98304000000 | bytes 14336000 | tf_op jit(solution)/shard_map/mixer_backward/pallas_call | solution.py:494
  277.7 15.7 %mixer_backward.3 = (bf16[1024,1664]{1,0:T(8,128)(2,1)}, f32[2,128,256]{2,1,0:T(8,128)}, f32[8,1024]{1,0:T(8,128)}, f32[4,1024]{1,0:T(4,128)}, f32[8,128]{1,0:T(8,128)}, /*index=5*/f32[1,512]{1,0:T(1,128)}) custom-call(f32[1024,128]{1,0:T(8,128)} %pad.18.places_ref, f32[1024,1664]{1,0:T(8,128)} %fusion.48.extra_ref.proj_ref, ...), custom_call_target="tpu_custom_call", output_to_operand_aliasing={{0}: (20, {})} | custom-call | flops 98304000000 | bytes 14336000 | tf_op jit(solution)/shard_map/mixer_backward/pallas_call | solution.py:494
  293.4 4.5 %collective-permute-done.50 = bf16[128,2048]{1,0:T(8,128)(2,1)S(1)} collective-permute-done((bf16[128,2048]{1,0:T(8,128)(2,1)S(1)}, bf16[128,2048]{1,0:T(8,128)(2,1)S(1)}, u32[]{:S(2)}, u32[]{:S(2)}) %collective-permute-start.50) | collective-permute-done | bytes 524320 | tf_op jit(solution)/shard_map/ppermute | solution.py:723
  299.5 8.4 %convolution_convert_fusion.3 = bf16[1024,1024]{1,0:T(8,128)(2,1)} fusion(bf16[1024,1664]{1,0:T(8,128)(2,1)} %get-tuple-element.250, bf16[1024,1664]{1,0:T(8,128)(2,1)} %all-gather.2.cloned.1.call-done), kind=kOutput, calls=%fused_computation.10 | convolution fusion | flops 3490709504 | bytes 8912896 | tf_op jit(solution)/shard_map/dot_general | solution.py:715
  308.0 5.5 %convolution_convert_fusion.1 = bf16[512,1536]{1,0:T(8,128)(2,1)} fusion(bf16[1024,1664]{1,0:T(8,128)(2,1)} %get-tuple-element.250, pred[]{:T(512)S(6)} %eq.69, bf16[1024,128]{1,0:T(8,128)(2,1)} %get-tuple-element.312, bf16[1024,128]{1,0:T(8,128)(2,1)} %get-tuple-element.313, bf16[1024,128]{1,0:T(8,128)(2,1)} %get-tuple-element.314, ...), kind=kOutput, calls=%fused_computation.4 | convolution fusion | flops 1620312064 | bytes 6815745 | tf_op jit(solution)/shard_map/dot_general | solution.py:715
  318.6 4.2 %add_convert_fusion.1 = bf16[512,1536]{1,0:T(8,128)(2,1)S(1)} fusion(bf16[512,1536]{1,0:T(8,128)(2,1)} %collective-permute-done.52, bf16[1024,1664]{1,0:T(8,128)(2,1)} %get-tuple-element.250, pred[]{:T(512)S(6)} %eq.69, bf16[1024,128]{1,0:T(8,128)(2,1)S(1)} %copy-done.56, bf16[1024,128]{1,0:T(8,128)(2,1)S(1)} %copy-done.57, ...), kind=kOutput, calls=%fused_computation.2 | convolution fusion | flops 1621884928 | bytes 8388609 | tf_op jit(solution)/shard_map/dot_general | solution.py:715
  328.3 7.6 %collective-permute-done.61 = bf16[128,1536]{1,0:T(8,128)(2,1)S(1)} collective-permute-done((bf16[128,1536]{1,0:T(8,128)(2,1)S(1)}, bf16[128,1536]{1,0:T(8,128)(2,1)S(1)}, u32[]{:S(2)}, u32[]{:S(2)}) %collective-permute-start.61) | collective-permute-done | bytes 393248 | tf_op jit(solution)/shard_map/ppermute | solution.py:723
  335.9 8.0 %collective-permute-done.60 = bf16[128,1536]{1,0:T(8,128)(2,1)S(1)} collective-permute-done((bf16[128,1536]{1,0:T(8,128)(2,1)S(1)}, bf16[128,1536]{1,0:T(8,128)(2,1)S(1)}, u32[]{:S(2)}, u32[]{:S(2)}) %collective-permute-start.60) | collective-permute-done | bytes 393248 | tf_op jit(solution)/shard_map/ppermute | solution.py:723
  365.9 8.2 %collective-permute-done.63 = bf16[128,512]{1,0:T(8,128)(2,1)S(1)} collective-permute-done((bf16[128,512]{1,0:T(8,128)(2,1)S(1)}, bf16[128,512]{1,0:T(8,128)(2,1)S(1)}, u32[]{:S(2)}, u32[]{:S(2)}) %collective-permute-start.63) | collective-permute-done | bytes 131104 | tf_op jit(solution)/shard_map/ppermute | solution.py:789
  (449 shorter events, 147.6 us)
Async XLA Ops:
  7.2 51.1 %all-gather.2.cloned.1.call-start = ((), (), s32[]{:S(2)}) async-start(), calls=%async_computation.1 | async-start | bytes 3833856 | tf_op jit(solution)/shard_map/all_gather | solution.py:1079
  11.8 364.5 %reduce-scatter.2.cloned.1.call-start = ((), (), s32[]{:S(2)}) async-start(), calls=%async_computation.2 | async-start | bytes 2621440 | tf_op jit(solution)/shard_map/reduce_scatter | solution.py:1194
  20.4 23.7 %collective-permute-start.6 = (bf16[128,512]{0,1:T(8,128)(2,1)S(1)}, bf16[128,512]{0,1:T(8,128)(2,1)}, u32[]{:S(2)}, u32[]{:S(2)}) collective-permute-start(bf16[128,512]{0,1:T(8,128)(2,1)S(1)} %bitcast.124), channel_id=1, source_target_pairs={{0,3},{1,0},{2,1},{3,2},{4,7},{5,4},{6,5},{7,6},{8,11},{9,8},{10,9... | collective-permute-start | bytes 393224 | tf_op jit(solution)/shard_map/ppermute | solution.py:789
  25.8 22.3 %collective-permute-start.7 = (bf16[128,512]{0,1:T(8,128)(2,1)S(1)}, bf16[128,512]{0,1:T(8,128)(2,1)}, u32[]{:S(2)}, u32[]{:S(2)}) collective-permute-start(bf16[128,512]{0,1:T(8,128)(2,1)S(1)} %bitcast.125), channel_id=1, source_target_pairs={{0,2},{1,3},{2,0},{3,1},{4,6},{5,7},{6,4},{7,5},{8,10},{9,11},{10,... | collective-permute-start | bytes 393224 | tf_op jit(solution)/shard_map/ppermute | solution.py:789
  25.8 22.3 %collective-permute-start.8 = (bf16[128,512]{0,1:T(8,128)(2,1)S(1)}, bf16[128,512]{0,1:T(8,128)(2,1)}, u32[]{:S(2)}, u32[]{:S(2)}) collective-permute-start(bf16[128,512]{0,1:T(8,128)(2,1)S(1)} %bitcast.126), channel_id=1, source_target_pairs={{0,1},{1,2},{2,3},{3,0},{4,5},{5,6},{6,7},{7,4},{8,9},{9,10},{10,1... | collective-permute-start | bytes 393224 | tf_op jit(solution)/shard_map/ppermute | solution.py:789
  75.1 27.2 %collective-permute-start.10 = (bf16[3,704,128]{2,1,0:T(8,128)(2,1)S(1)}, bf16[3,704,128]{2,1,0:T(8,128)(2,1)S(1)}, u32[]{:S(2)}, u32[]{:S(2)}) collective-permute-start(bf16[3,704,128]{2,1,0:T(8,128)(2,1)S(1)} %pad_maximum_fusion.8), channel_id=1, source_target_pairs={{1,0},{0,2},{2,3},{3,1},{5,4},{4,6},{6,7},{7,5},{9,8},{8,10},{10,1... | collective-permute-start | bytes 1622024 | tf_op jit(solution)/shard_map/ppermute | solution.py:955
  76.4 26.0 %collective-permute-start.11 = (bf16[3,704,128]{2,1,0:T(8,128)(2,1)S(1)}, bf16[3,704,128]{2,1,0:T(8,128)(2,1)S(1)}, u32[]{:S(2)}, u32[]{:S(2)}) collective-permute-start(bf16[3,704,128]{2,1,0:T(8,128)(2,1)S(1)} %pad_maximum_fusion.8), channel_id=1, source_target_pairs={{2,1},{1,2},{6,5},{5,6},{10,9},{9,10},{14,13},{13,14},{18,17},{17,... | collective-permute-start | bytes 1622024 | tf_op jit(solution)/shard_map/ppermute | solution.py:956
  77.6 24.7 %collective-permute-start.12 = (bf16[128,2048]{0,1:T(8,128)(2,1)S(1)}, bf16[128,2048]{0,1:T(8,128)(2,1)S(1)}, u32[]{:S(2)}, u32[]{:S(2)}) collective-permute-start(bf16[128,2048]{0,1:T(8,128)(2,1)S(1)} %pad_maximum_fusion.9), channel_id=1, source_target_pairs={{0,8},{4,12},{8,0},{12,4},{16,24},{20,28},{24,16},{28,20},{1,9},{5... | collective-permute-start | bytes 1572872 | tf_op jit(solution)/shard_map/ppermute | solution.py:723
  79.2 23.1 %collective-permute-start.13 = (bf16[128,2048]{0,1:T(8,128)(2,1)S(1)}, bf16[128,2048]{0,1:T(8,128)(2,1)S(1)}, u32[]{:S(2)}, u32[]{:S(2)}) collective-permute-start(bf16[128,2048]{0,1:T(8,128)(2,1)S(1)} %pad_maximum_fusion.9), channel_id=1, source_target_pairs={{0,16},{4,20},{8,24},{12,28},{16,0},{20,4},{24,8},{28,12},{1,17},{... | collective-permute-start | bytes 1572872 | tf_op jit(solution)/shard_map/ppermute | solution.py:723
  103.7 49.0 %collective-permute-start.22 = (bf16[128,2048]{0,1:T(8,128)(2,1)S(1)}, bf16[128,2048]{0,1:T(8,128)(2,1)S(1)}, u32[]{:S(2)}, u32[]{:S(2)}) collective-permute-start(bf16[128,2048]{0,1:T(8,128)(2,1)S(1)} %pad_maximum_fusion.9), channel_id=1, source_target_pairs={{0,4},{4,0},{8,12},{12,8},{16,20},{20,16},{24,28},{28,24},{1,5},{5... | collective-permute-start | bytes 1572872 | tf_op jit(solution)/shard_map/ppermute | solution.py:723
  127.5 22.9 %collective-permute-start.20 = (bf16[256,512]{1,0:T(8,128)(2,1)S(1)}, bf16[256,512]{1,0:T(8,128)(2,1)S(1)}, u32[]{:S(2)}, u32[]{:S(2)}) collective-permute-start(bf16[256,512]{1,0:T(8,128)(2,1)S(1)} %get-tuple-element.344), channel_id=1, source_target_pairs={{0,2},{1,3},{2,0},{3,1},{4,6},{5,7},{6,4},{7,5},{8,10},{9,11},{10,... | collective-permute-start | bytes 786440 | tf_op jit(solution)/shard_map/ppermute | solution.py:789
  127.5 22.8 %collective-permute-start.21 = (bf16[256,512]{1,0:T(8,128)(2,1)S(1)}, bf16[256,512]{1,0:T(8,128)(2,1)S(1)}, u32[]{:S(2)}, u32[]{:S(2)}) collective-permute-start(bf16[256,512]{1,0:T(8,128)(2,1)S(1)} %get-tuple-element.343), channel_id=1, source_target_pairs={{0,1},{1,2},{2,3},{3,0},{4,5},{5,6},{6,7},{7,4},{8,9},{9,10},{10,1... | collective-permute-start | bytes 786440 | tf_op jit(solution)/shard_map/ppermute | solution.py:789
  129.7 42.5 %collective-permute-start.30 = (bf16[2,3,704,128]{3,2,1,0:T(8,128)(2,1)S(1)}, bf16[2,3,704,128]{3,2,1,0:T(8,128)(2,1)}, u32[]{:S(2)}, u32[]{:S(2)}) collective-permute-start(bf16[2,3,704,128]{3,2,1,0:T(8,128)(2,1)S(1)} %pad_maximum_fusion.1.refs_8_), channel_id=1, source_target_pairs={{0,16},{4,20},{8,24},{12,28},{16,0},{20,4},{24,8},{28,12},{1,17},{... | collective-permute-start | bytes 3244040 | tf_op jit(solution)/shard_map/ppermute | solution.py:723
  134.3 37.9 %collective-permute-start.31 = (bf16[2,3,704,128]{3,2,1,0:T(8,128)(2,1)S(1)}, bf16[2,3,704,128]{3,2,1,0:T(8,128)(2,1)}, u32[]{:S(2)}, u32[]{:S(2)}) collective-permute-start(bf16[2,3,704,128]{3,2,1,0:T(8,128)(2,1)S(1)} %pad_maximum_fusion.2.refs_10_), channel_id=1, source_target_pairs={{0,8},{4,12},{8,0},{12,4},{16,24},{20,28},{24,16},{28,20},{1,9},{5... | collective-permute-start | bytes 3244040 | tf_op jit(solution)/shard_map/ppermute | solution.py:723
  212.5 25.1 %collective-permute-start.38 = (bf16[2,3,704,128]{3,2,1,0:T(8,128)(2,1)S(1)}, bf16[2,3,704,128]{3,2,1,0:T(8,128)(2,1)S(1)}, u32[]{:S(2)}, u32[]{:S(2)}) collective-permute-start(bf16[2,3,704,128]{3,2,1,0:T(8,128)(2,1)S(1)} %pad_maximum_fusion.3), channel_id=1, source_target_pairs={{0,8},{4,12},{8,0},{12,4},{16,24},{20,28},{24,16},{28,20},{1,9},{5... | collective-permute-start | bytes 3244040 | tf_op jit(solution)/shard_map/ppermute | solution.py:723
  213.2 24.9 %collective-permute-start.39 = (bf16[2,3,704,128]{3,2,1,0:T(8,128)(2,1)S(1)}, bf16[2,3,704,128]{3,2,1,0:T(8,128)(2,1)S(1)}, u32[]{:S(2)}, u32[]{:S(2)}) collective-permute-start(bf16[2,3,704,128]{3,2,1,0:T(8,128)(2,1)S(1)} %slice.212), channel_id=1, source_target_pairs={{0,16},{4,20},{8,24},{12,28},{16,0},{20,4},{24,8},{28,12},{1,17},{... | collective-permute-start | bytes 3244040 | tf_op jit(solution)/shard_map/ppermute | solution.py:723
  218.8 24.9 %collective-permute-start.35 = (bf16[256,512]{1,0:T(8,128)(2,1)S(1)}, bf16[256,512]{1,0:T(8,128)(2,1)S(1)}, u32[]{:S(2)}, u32[]{:S(2)}) collective-permute-start(bf16[256,512]{1,0:T(8,128)(2,1)S(1)} %get-tuple-element.341), channel_id=1, source_target_pairs={{0,1},{1,2},{2,3},{3,0},{4,5},{5,6},{6,7},{7,4},{8,9},{9,10},{10,1... | collective-permute-start | bytes 786440 | tf_op jit(solution)/shard_map/ppermute | solution.py:789
  219.3 24.4 %collective-permute-start.36 = (bf16[256,512]{1,0:T(8,128)(2,1)S(1)}, bf16[256,512]{1,0:T(8,128)(2,1)S(1)}, u32[]{:S(2)}, u32[]{:S(2)}) collective-permute-start(bf16[256,512]{1,0:T(8,128)(2,1)S(1)} %get-tuple-element.340), channel_id=1, source_target_pairs={{0,2},{1,3},{2,0},{3,1},{4,6},{5,7},{6,4},{7,5},{8,10},{9,11},{10,... | collective-permute-start | bytes 786440 | tf_op jit(solution)/shard_map/ppermute | solution.py:789
  238.1 27.8 %collective-permute-start.41 = (bf16[256,1024]{1,0:T(8,128)(2,1)}, bf16[256,1024]{1,0:T(8,128)(2,1)}, u32[]{:S(2)}, u32[]{:S(2)}) collective-permute-start(bf16[256,1024]{1,0:T(8,128)(2,1)} %get-tuple-element.227), channel_id=1, source_target_pairs={{0,4},{4,0},{8,12},{12,8},{16,20},{20,16},{24,28},{28,24},{1,5},{5... | collective-permute-start | bytes 1572872 | tf_op jit(solution)/shard_map/ppermute | solution.py:723
  242.7 24.6 %collective-permute-start.45 = (bf16[512,2048]{1,0:T(8,128)(2,1)}, bf16[512,2048]{1,0:T(8,128)(2,1)}, u32[]{:S(2)}, u32[]{:S(2)}) collective-permute-start(bf16[512,2048]{1,0:T(8,128)(2,1)} %convolution_convert_fusion), channel_id=1, source_target_pairs={{0,4},{4,0},{8,12},{12,8},{16,20},{20,16},{24,28},{28,24},{1,5},{5... | collective-permute-start | bytes 6291464 | tf_op jit(solution)/shard_map/ppermute | solution.py:723
  243.8 23.5 %collective-permute-start.42 = (bf16[256,1024]{1,0:T(8,128)(2,1)}, bf16[256,1024]{1,0:T(8,128)(2,1)}, u32[]{:S(2)}, u32[]{:S(2)}) collective-permute-start(bf16[256,1024]{1,0:T(8,128)(2,1)} %add_convert_fusion.8), channel_id=1, source_target_pairs={{0,1},{1,0},{2,3},{3,2},{4,5},{5,4},{6,7},{7,6},{8,9},{9,8},{10,11... | collective-permute-start | bytes 1572872 | tf_op jit(solution)/shard_map/ppermute | solution.py:723
  244.7 22.6 %collective-permute-start.43 = (bf16[3,704,128]{2,1,0:T(8,128)(2,1)}, bf16[3,704,128]{2,1,0:T(8,128)(2,1)}, u32[]{:S(2)}, u32[]{:S(2)}) collective-permute-start(bf16[3,704,128]{2,1,0:T(8,128)(2,1)} %get-tuple-element.229), channel_id=1, source_target_pairs={{0,16},{4,20},{8,24},{12,28},{16,0},{20,4},{24,8},{28,12},{1,17},{... | collective-permute-start | bytes 1622024 | tf_op jit(solution)/shard_map/ppermute | solution.py:723
  272.6 25.3 %collective-permute-start.50 = (bf16[128,2048]{1,0:T(8,128)(2,1)S(1)}, bf16[128,2048]{1,0:T(8,128)(2,1)S(1)}, u32[]{:S(2)}, u32[]{:S(2)}) collective-permute-start(bf16[128,2048]{1,0:T(8,128)(2,1)S(1)} %get-tuple-element.320), channel_id=1, source_target_pairs={{0,16},{4,20},{8,24},{12,28},{16,0},{20,4},{24,8},{28,12},{1,17},{... | collective-permute-start | bytes 1572872 | tf_op jit(solution)/shard_map/ppermute | solution.py:723
  273.4 24.5 %collective-permute-start.51 = (bf16[128,2048]{1,0:T(8,128)(2,1)S(1)}, bf16[128,2048]{1,0:T(8,128)(2,1)S(1)}, u32[]{:S(2)}, u32[]{:S(2)}) collective-permute-start(bf16[128,2048]{1,0:T(8,128)(2,1)S(1)} %get-tuple-element.319), channel_id=1, source_target_pairs={{0,24},{4,28},{8,16},{12,20},{16,8},{20,12},{24,0},{28,4},{1,25},{... | collective-permute-start | bytes 1572872 | tf_op jit(solution)/shard_map/ppermute | solution.py:723
  (142 other events, 1438.2 us)
Sparse Core Ops, SparseCore 0:
  11.9 36.1 all-gather.1
  317.0 48.4 reduce-scatter.1

commit v2 on v1

--- a/solution.py
+++ b/solution.py
@@ -27,20 +27,25 @@
 bf16 = jnp.bfloat16
 
 
-def dot(a, b, dims, passes):
+def dot(a, b, dims, passes, join=False):
     if passes == 6:
         return lax.dot_general(
             a, b, (dims, ((), ())), precision=lax.Precision.HIGHEST, preferred_element_type=f32
         )
     a_hi = a.astype(bf16)
     b_hi = b.astype(bf16)
-    out = lax.dot_general(a_hi, b_hi, (dims, ((), ())), preferred_element_type=f32)
-    if passes == 3:
-        a_lo = (a - a_hi.astype(f32)).astype(bf16)
-        b_lo = (b - b_hi.astype(f32)).astype(bf16)
-        out = out + lax.dot_general(a_hi, b_lo, (dims, ((), ())), preferred_element_type=f32)
-        out = out + lax.dot_general(a_lo, b_hi, (dims, ((), ())), preferred_element_type=f32)
-    return out
+    product = lambda x, y: lax.dot_general(x, y, (dims, ((), ())), preferred_element_type=f32)
+    if passes == 1:
+        return product(a_hi, b_hi)
+    a_lo = (a - a_hi.astype(f32)).astype(bf16)
+    b_lo = (b - b_hi.astype(f32)).astype(bf16)
+    (a_dim,), (b_dim,) = dims
+    if not join:
+        return product(a_hi, b_hi) + product(a_hi, b_lo) + product(a_lo, b_hi)
+    both = product(
+        jnp.concatenate([a_hi, a_lo], a_dim), jnp.concatenate([b_hi, b_hi], b_dim)
+    )
+    return both + product(a_hi, b_lo)
 
 
 def exact_left(mask, b):
@@ -130,9 +135,9 @@
     while size < CHUNK:
         part = ((row // (2 * size)) == (col // (2 * size))) & ((row // size) != (col // size))
         steps = [
-            dot(jnp.where(part, lower, 0.0), inv, NN, passes) for lower, inv in zip(lowers, invs)
+            dot(jnp.where(part, lower, 0.0), inv, NN, passes, True) for lower, inv in zip(lowers, invs)
         ]
-        invs = [inv - dot(inv, step, NN, passes) for inv, step in zip(invs, steps)]
+        invs = [inv - dot(inv, step, NN, passes, True) for inv, step in zip(invs, steps)]
         size *= 2
     return invs
 
@@ -200,7 +205,7 @@
             decay, strict, beta_col, carried, end, carried_last = head_scalars(
                 h, heads, infos[u], beta, total, across
             )
-            inner = dot(jnp.concatenate([key, query], 0), key, NT, prec["kk"])
+            inner = dot(jnp.concatenate([key, query], 0), key, NT, prec["kk"], True)
             kk = inner[:CHUNK]
             qk = inner[CHUNK:]
             kk_ref[u, h] = kk
@@ -216,7 +221,7 @@
         own = slice(u * CHUNK, (u + 1) * CHUNK)
         lower, sides, reads_q, attend, ends, carried_last = first[at]
         solve_ref[u, h] = inv
-        solved = dot(inv, sides, NN, prec["solve"])
+        solved = dot(inv, sides, NN, prec["solve"], True)
         across_ref[own, h * DK : (h + 1) * DK] = solved[:, DV:]
         ready[at] = (
             jnp.concatenate([reads_q, solved[:, DV:]], 0), solved[:, :DV], attend, ends,
@@ -228,10 +233,10 @@
             readers, fixed, attend, ends, carried_last = ready[u, h]
             state = state_ref[h]
             state_out_ref[u, h] = state
-            reads = dot(readers, state, NN, prec["state"])
+            reads = dot(readers, state, NN, prec["state"], True)
             delta = fixed - reads[CHUNK:]
-            state_ref[h] = carried_last * state + dot(ends, delta, TN, prec["state"])
-            result = reads[:CHUNK] + dot(attend, delta, NN, prec["attend"])
+            state_ref[h] = carried_last * state + dot(ends, delta, TN, prec["state"], True)
+            result = reads[:CHUNK] + dot(attend, delta, NN, prec["attend"], True)
             delta_ref[own, h * DV : (h + 1) * DV] = delta
             out_ref[own, h * DV : (h + 1) * DV] = result
             gate = proj_ref[own, h * MIX + CONV : (h + 1) * MIX]
@@ -1194,9 +1199,8 @@
     grad_normed_one = lax.psum_scatter(
         sent, "tensor", scatter_dimension=0, tiled=True
     ).astype(f32)
-    grad_proj = after(grad_proj, sent)
+    grad_proj, again = after((grad_proj, sent), sent)
     grad_in = PlaneSum(rows_one, grad_proj[:, :wide])
-    grad_in.send()
     head_full = lax.dynamic_update_slice_in_dim(
         jnp.zeros((2, all_heads), f32),
         grad_head[:2, BETA_AT + heads : BETA_AT + 2 * heads],
@@ -1208,14 +1212,16 @@
     ends = [sum(sizes[:i]) for i in range(5)]
     at = BETA_AT + 2 * heads
     grad_small = product(rows_one, grad_proj[:, wide:], TN)[:, BETA_AT:at]
-    again = after(sent, grad_in.total)
     gain_one = jnp.sum(again.astype(f32) * rows_one.astype(f32), 0) / gains[0]
     parts = [
         gain_one, grad_gain_two, head_full.reshape(-1), grad_conv.reshape(-1),
         grad_onorm.reshape(-1), grad_small.T.reshape(-1),
     ]
-    totals = sum_over(jnp.concatenate(parts), "dp")
-    shared = totals[: sizes[0]]
+    totals, grad_in.came = lax.optimization_barrier(
+        (sum_over(jnp.concatenate(parts), "dp"), grad_in.came)
+    )
+    grad_in.send()
+    shared = after(totals[: sizes[0]], grad_in.parts)
     shared = sum(ordered(swap_parts(lambda i: shared, "tensor"), "tensor"))
     out_parts = after(out_sum.finish().astype(bf16), grad_in.total)
     out_out = sum(block.astype(f32) for block in out_weights.send_sum(out_parts, width))

time: 391 us -> 387 us (0.990)
  waiting for transfers between devices: 101 us -> 95 us
  matrix products: 32.6 us -> 28.6 us
    dot_general x9, matrix products: 32.6 us -> 28.6 us  [product(): lax.dot_general(left, right, (dims, ((), ())), preferred_element_type=f32)]
    unnamed x202 -> x174, local copies, waits for them, and re-layouts: 8.34 us -> 8.57 us
  transfers between devices with their start and end apart: 67 -> 67, of which waited for: 20 -> 22; matrix products, arithmetic and copies ran while one was open for 16% -> 19% of each run, Pallas kernels for 18% -> 18%
where the time goes in v2:
time: 387 us; the launch traced here: 383 us
  waiting for transfers between devices  95 us (25%)
  starting transfers between devices  86.6 us (22%)
  Pallas kernels  86.6 us (22%)
  local copies, waits for them, and re-layouts  38.8 us (10%)
  other arithmetic  31.3 us (8%)
  matrix products  28.6 us (7%)
  between operations  16 us (4%)
    ppermute x40, waiting for transfers between devices, exchange(): lax.ppermute(x, axis, [(i, i ^ bit) for i in range(lax.axis_size(axis))])  53.1 us
    pallas_call x2, Pallas kernels, mixer_backward(): pl.pallas_call(functools.partial(backward_body, heads, prec), grid=(steps...  31 us
    ppermute x40, starting transfers between devices, exchange(): lax.ppermute(x, axis, [(i, i ^ bit) for i in range(lax.axis_size(axis))])  29.7 us
    dot_general x9, matrix products, product(): lax.dot_general(left, right, (dims, ((), ())), preferred_element_type=f32)  28.6 us
    ppermute x15, starting transfers between devices, shifted(): return lax.ppermute(x, axis, [(i, (i + by) % ways) for i in range(ways)])  28.3 us
    ppermute x15, waiting for transfers between devices, shifted(): return lax.ppermute(x, axis, [(i, (i + by) % ways) for i in range(ways)])  28.1 us
    pallas_call x2, Pallas kernels, mixer_forward(): pl.pallas_call(functools.partial(forward_body, heads, prec), grid=(steps,...  25.7 us
    ppermute x3, starting transfers between devices, line_gather(): below.append(lax.ppermute(below[-1], axis, up))  21.6 us
  transfers between devices with their start and end apart: 67, of which 22 were waited for; matrix products, arithmetic and copies ran while one was open for 19% of the time, Pallas kernels for 18%

profile of v2, /device:TPU:0, one launch (start us, length us, event | category | flops | bytes accessed | tf_op | source)
XLA Modules:
  0.0 382.8 jit_solution(17910651494806186008)
XLA Ops:
  13.9 5.1 %collective-permute-start = (bf16[256,1024]{1,0:T(8,128)(2,1)S(1)}, bf16[256,1024]{1,0:T(8,128)(2,1)S(1)}, u32[]{:S(2)}, u32[]{:S(2)}) collective-permute-start(bf16[256,1024]{1,0:T(8,128)(2,1)S(1)} %fusion.8), channel_id=1, source_target_pairs={{0,1},{1,2},{2,3},{4,5},{5,6},{6,7},{8,9},{9,10},{10,11},{12,13},{... | collective-permute-start | bytes 1572872 | tf_op jit(solution)/shard_map/ppermute | solution.py:750
  20.3 4.7 %collective-permute-start.6 = (bf16[128,512]{0,1:T(8,128)(2,1)S(1)}, bf16[128,512]{0,1:T(8,128)(2,1)S(1)}, u32[]{:S(2)}, u32[]{:S(2)}) collective-permute-start(bf16[128,512]{0,1:T(8,128)(2,1)S(1)} %bitcast.124), channel_id=1, source_target_pairs={{0,3},{1,0},{2,1},{3,2},{4,7},{5,4},{6,5},{7,6},{8,11},{9,8},{10,9... | collective-permute-start | bytes 393224 | tf_op jit(solution)/shard_map/ppermute | solution.py:794
  27.8 3.5 collective-permute-done
  31.3 9.5 %collective-permute-start.1 = (bf16[256,1024]{1,0:T(8,128)(2,1)S(1)}, bf16[256,1024]{1,0:T(8,128)(2,1)}, u32[]{:S(2)}, u32[]{:S(2)}) collective-permute-start(bf16[256,1024]{1,0:T(8,128)(2,1)S(1)} %collective-permute-done), channel_id=1, source_target_pairs={{0,1},{1,2},{2,3},{4,5},{5,6},{6,7},{8,9},{9,10},{10,11},{12,13},{... | collective-permute-start | bytes 1572872 | tf_op jit(solution)/shard_map/ppermute | solution.py:750
  44.2 3.9 %collective-permute-done.7 = bf16[128,512]{0,1:T(8,128)(2,1)} collective-permute-done((bf16[128,512]{0,1:T(8,128)(2,1)S(1)}, bf16[128,512]{0,1:T(8,128)(2,1)}, u32[]{:S(2)}, u32[]{:S(2)}) %collective-permute-start.7) | collective-permute-done | bytes 131104 | tf_op jit(solution)/shard_map/ppermute | solution.py:794
  49.9 7.0 %collective-permute-start.2 = (bf16[256,1024]{1,0:T(8,128)(2,1)}, bf16[256,1024]{1,0:T(8,128)(2,1)}, u32[]{:S(2)}, u32[]{:S(2)}) collective-permute-start(bf16[256,1024]{1,0:T(8,128)(2,1)} %collective-permute-done.1), channel_id=1, source_target_pairs={{0,1},{1,2},{2,3},{4,5},{5,6},{6,7},{8,9},{9,10},{10,11},{12,13},{... | collective-permute-start | bytes 1572872 | tf_op jit(solution)/shard_map/ppermute | solution.py:750
  62.3 4.5 %collective-permute-done.2 = bf16[256,1024]{1,0:T(8,128)(2,1)} collective-permute-done((bf16[256,1024]{1,0:T(8,128)(2,1)}, bf16[256,1024]{1,0:T(8,128)(2,1)}, u32[]{:S(2)}, u32[]{:S(2)}) %collective-permute-start.2) | collective-permute-done | bytes 524320 | tf_op jit(solution)/shard_map/ppermute | solution.py:750
  66.7 5.0 %collective-permute-done.5 = bf16[256,1024]{1,0:T(8,128)(2,1)} collective-permute-done((bf16[256,1024]{1,0:T(8,128)(2,1)}, bf16[256,1024]{1,0:T(8,128)(2,1)}, u32[]{:S(2)}, u32[]{:S(2)}) %collective-permute-start.5) | collective-permute-done | bytes 524320 | tf_op jit(solution)/shard_map/ppermute | solution.py:751
  80.3 5.8 %fusion.46.extra_ref.proj_ref = f32[1024,1664]{1,0:T(8,128)} fusion(bf16[1024,1024]{1,0:T(8,128)(2,1)S(1)} %pad_maximum_fusion, bf16[1024,1664]{1,0:T(8,128)(2,1)S(1)} %copy-done.66), kind=kOutput, calls=%fused_computation.170 | convolution fusion | flops 3489660928 | bytes 12320768 | tf_op jit(solution)/shard_map/dot_general | solution.py:720
  87.5 12.9 %mixer_forward.2 = (bf16[1024,512]{1,0:T(8,128)(2,1)}, f32[1024,1024]{1,0:T(8,128)}, f32[1024,512]{1,0:T(8,128)}, f32[1024,512]{1,0:T(8,128)}, f32[1024,256]{1,0...) custom-call(f32[1024,128]{1,0:T(8,128)} %pad.18.places_ref, ...), custom_call_target="tpu_custom_call" | custom-call | flops 65536000000 | bytes 12288000 | tf_op jit(solution)/shard_map/mixer_forward/pallas_call | solution.py:444
  107.4 12.9 %mixer_forward.3 = (bf16[1024,512]{1,0:T(8,128)(2,1)}, f32[1024,1024]{1,0:T(8,128)}, f32[1024,512]{1,0:T(8,128)}, f32[1024,512]{1,0:T(8,128)}, f32[1024,256]{1,0...) custom-call(f32[1024,128]{1,0:T(8,128)} %pad.18.places_ref, ...), custom_call_target="tpu_custom_call", output_to_operand_aliasing={{0}: (8, {}), {1}: (9, {}), {2}: (10, {}), {3}: (11, {}), {... | custom-call | flops 65536000000 | bytes 12288000 | tf_op jit(solution)/shard_map/mixer_forward/pallas_call | solution.py:444
  132.6 14.7 %collective-permute-done.20 = bf16[256,512]{1,0:T(8,128)(2,1)S(1)} collective-permute-done((bf16[256,512]{1,0:T(8,128)(2,1)S(1)}, bf16[256,512]{1,0:T(8,128)(2,1)S(1)}, u32[]{:S(2)}, u32[]{:S(2)}) %collective-permute-start.20) | collective-permute-done | bytes 262176 | tf_op jit(solution)/shard_map/ppermute | solution.py:794
  154.8 13.4 %collective-permute-done.27.refs_2_ = bf16[256,1024]{1,0:T(8,128)(2,1)} collective-permute-done((bf16[256,1024]{1,0:T(8,128)(2,1)S(1)}, bf16[256,1024]{1,0:T(8,128)(2,1)}, u32[]{:S(2)}, u32[]{:S(2)}) %collective-permute-start.27) | collective-permute-done | bytes 524320 | tf_op jit(solution)/shard_map/ppermute | solution.py:728
  170.4 18.8 %ffn_both.1 = (bf16[1024,704]{1,0:T(8,128)(2,1)}, bf16[1024,704]{1,0:T(8,128)(2,1)}, bf16[1024,704]{1,0:T(8,128)(2,1)}, bf16[256,1024]{1,0:T(8,128)(2,1)}, bf16[...) custom-call(s32[1]{0:T(128)} %bitcast.34.place_ref, ...), custom_call_target="tpu_custom_call" | custom-call | flops 17716740096 | bytes 8388608 | tf_op jit(solution)/shard_map/ffn_both/pallas_call | solution.py:634
  193.3 11.0 %ffn_weight_grads.1 = (bf16[4,3,704,128]{3,2,1,0:T(8,128)(2,1)}, bf16[4,3,704,128]{3,2,1,0:T(8,128)(2,1)}) custom-call(s32[1]{0:T(128)} %bitcast.34.place_ref, bf16[256,1024]{1,0:T(8,128)(2,1)} %copy-done.43, bf16[256,1024]{1,0:T(8,128)(2,1)} %collective-permute-done.26.refs_1_, bf16[256,1024]{1,0:T(8,128)(2,1)} %collective-permute-done.27.refs_2_, ...), custom_call_target="tpu_custom_call" | custom-call | flops 8858370048 | bytes 8388608 | tf_op jit(solution)/shard_map/ffn_weight_grads/pallas_call | solution.py:687
  220.0 13.5 %collective-permute-done.38 = bf16[2,3,704,128]{3,2,1,0:T(8,128)(2,1)S(1)} collective-permute-done((bf16[2,3,704,128]{3,2,1,0:T(8,128)(2,1)S(1)}, bf16[2,3,704,128]{3,2,1,0:T(8,128)(2,1)S(1)}, u32[]{:S(2)}, u32[]{:S(2)}) %collective-permute-start.38) | collective-permute-done | bytes 1081376 | tf_op jit(solution)/shard_map/ppermute | solution.py:728
  246.2 15.5 %mixer_backward.2 = (bf16[1024,1664]{1,0:T(8,128)(2,1)}, f32[2,128,256]{2,1,0:T(8,128)}, f32[8,1024]{1,0:T(8,128)}, f32[4,1024]{1,0:T(4,128)}, f32[8,128]{1,0:T(8,128)}, /*index=5*/f32[1,512]{1,0:T(1,128)}) custom-call(f32[1024,128]{1,0:T(8,128)} %pad.18.places_ref, f32[1024,1664]{1,0:T(8,128)} %fusion.46.extra_ref.proj_ref, ...), custom_call_target="tpu_custom_call" | custom-call | flops 98304000000 | bytes 14336000 | tf_op jit(solution)/shard_map/mixer_backward/pallas_call | solution.py:499
  276.3 15.5 %mixer_backward.3 = (bf16[1024,1664]{1,0:T(8,128)(2,1)}, f32[2,128,256]{2,1,0:T(8,128)}, f32[8,1024]{1,0:T(8,128)}, f32[4,1024]{1,0:T(4,128)}, f32[8,128]{1,0:T(8,128)}, /*index=5*/f32[1,512]{1,0:T(1,128)}) custom-call(f32[1024,128]{1,0:T(8,128)} %pad.18.places_ref, f32[1024,1664]{1,0:T(8,128)} %fusion.46.extra_ref.proj_ref, ...), custom_call_target="tpu_custom_call", output_to_operand_aliasing={{0}: (20, {})} | custom-call | flops 98304000000 | bytes 14336000 | tf_op jit(solution)/shard_map/mixer_backward/pallas_call | solution.py:499
  296.1 8.3 %convolution_convert_fusion.3 = bf16[1024,1024]{1,0:T(8,128)(2,1)} fusion(bf16[1024,1664]{1,0:T(8,128)(2,1)} %get-tuple-element.257, bf16[1024,1664]{1,0:T(8,128)(2,1)} %all-gather.2.cloned.1.call-done), kind=kOutput, calls=%fused_computation.10 | convolution fusion | flops 3490709504 | bytes 8912896 | tf_op jit(solution)/shard_map/dot_general | solution.py:720
  310.2 3.9 %convolution_convert_fusion.1 = bf16[512,1536]{1,0:T(8,128)(2,1)S(1)} fusion(bf16[1024,1664]{1,0:T(8,128)(2,1)} %get-tuple-element.257, pred[]{:T(512)S(6)} %eq.69, bf16[1024,128]{1,0:T(8,128)(2,1)S(1)} %copy-done.46, bf16[1024,128]{1,0:T(8,128)(2,1)S(1)} %copy-done.47, bf16[1024,128]{1,0:T(8,128)(2,1)S(1)} %copy-done.48, ...), kind=kOutput, calls=%fused_computation.4 | convolution fusion | flops 1620312064 | bytes 6815745 | tf_op jit(solution)/shard_map/dot_general | solution.py:720
  334.2 6.7 %collective-permute-done.56 = bf16[128,1536]{1,0:T(8,128)(2,1)S(1)} collective-permute-done((bf16[128,1536]{1,0:T(8,128)(2,1)}, bf16[128,1536]{1,0:T(8,128)(2,1)S(1)}, u32[]{:S(2)}, u32[]{:S(2)}) %collective-permute-start.56) | collective-permute-done | bytes 393248 | tf_op jit(solution)/shard_map/ppermute | solution.py:728
  340.9 7.3 %collective-permute-done.57 = bf16[128,1536]{1,0:T(8,128)(2,1)S(1)} collective-permute-done((bf16[128,1536]{1,0:T(8,128)(2,1)}, bf16[128,1536]{1,0:T(8,128)(2,1)S(1)}, u32[]{:S(2)}, u32[]{:S(2)}) %collective-permute-start.57) | collective-permute-done | bytes 393248 | tf_op jit(solution)/shard_map/ppermute | solution.py:728
  349.7 6.0 %collective-permute-start.60 = (f32[2064]{0:T(1024)S(1)}, f32[2064]{0:T(1024)S(1)}, u32[]{:S(2)}, u32[]{:S(2)}) collective-permute-start(f32[2064]{0:T(1024)S(1)} %slice.241), channel_id=1, source_target_pairs={{0,2},{1,3},{2,0},{3,1},{4,6},{5,7},{6,4},{7,5},{8,10},{9,11},{10,... | collective-permute-start | bytes 24776 | tf_op jit(solution)/shard_map/ppermute | solution.py:794
  366.2 4.8 %collective-permute-done.63 = bf16[128,512]{1,0:T(8,128)(2,1)S(1)} collective-permute-done((bf16[128,512]{1,0:T(8,128)(2,1)S(1)}, bf16[128,512]{1,0:T(8,128)(2,1)S(1)}, u32[]{:S(2)}, u32[]{:S(2)}) %collective-permute-start.63) | collective-permute-done | bytes 131104 | tf_op jit(solution)/shard_map/ppermute | solution.py:794
  (422 shorter events, 152.6 us)
Async XLA Ops:
  7.2 51.0 %all-gather.2.cloned.1.call-start = ((), (), s32[]{:S(2)}) async-start(), calls=%async_computation.1 | async-start | bytes 3833856 | tf_op jit(solution)/shard_map/all_gather | solution.py:1084
  11.8 360.1 %reduce-scatter.2.cloned.1.call-start = ((), (), s32[]{:S(2)}) async-start(), calls=%async_computation.2 | async-start | bytes 2621440 | tf_op jit(solution)/shard_map/reduce_scatter | solution.py:1199
  20.3 23.7 %collective-permute-start.6 = (bf16[128,512]{0,1:T(8,128)(2,1)S(1)}, bf16[128,512]{0,1:T(8,128)(2,1)S(1)}, u32[]{:S(2)}, u32[]{:S(2)}) collective-permute-start(bf16[128,512]{0,1:T(8,128)(2,1)S(1)} %bitcast.124), channel_id=1, source_target_pairs={{0,3},{1,0},{2,1},{3,2},{4,7},{5,4},{6,5},{7,6},{8,11},{9,8},{10,9... | collective-permute-start | bytes 393224 | tf_op jit(solution)/shard_map/ppermute | solution.py:794
  25.1 23.0 %collective-permute-start.7 = (bf16[128,512]{0,1:T(8,128)(2,1)S(1)}, bf16[128,512]{0,1:T(8,128)(2,1)}, u32[]{:S(2)}, u32[]{:S(2)}) collective-permute-start(bf16[128,512]{0,1:T(8,128)(2,1)S(1)} %bitcast.125), channel_id=1, source_target_pairs={{0,2},{1,3},{2,0},{3,1},{4,6},{5,7},{6,4},{7,5},{8,10},{9,11},{10,... | collective-permute-start | bytes 393224 | tf_op jit(solution)/shard_map/ppermute | solution.py:794
  25.1 23.0 %collective-permute-start.8 = (bf16[128,512]{0,1:T(8,128)(2,1)S(1)}, bf16[128,512]{0,1:T(8,128)(2,1)}, u32[]{:S(2)}, u32[]{:S(2)}) collective-permute-start(bf16[128,512]{0,1:T(8,128)(2,1)S(1)} %bitcast.126), channel_id=1, source_target_pairs={{0,1},{1,2},{2,3},{3,0},{4,5},{5,6},{6,7},{7,4},{8,9},{9,10},{10,1... | collective-permute-start | bytes 393224 | tf_op jit(solution)/shard_map/ppermute | solution.py:794
  74.5 26.4 %collective-permute-start.10 = (bf16[3,704,128]{2,1,0:T(8,128)(2,1)S(1)}, bf16[3,704,128]{2,1,0:T(8,128)(2,1)S(1)}, u32[]{:S(2)}, u32[]{:S(2)}) collective-permute-start(bf16[3,704,128]{2,1,0:T(8,128)(2,1)S(1)} %pad_maximum_fusion.8), channel_id=1, source_target_pairs={{1,0},{0,2},{2,3},{3,1},{5,4},{4,6},{6,7},{7,5},{9,8},{8,10},{10,1... | collective-permute-start | bytes 1622024 | tf_op jit(solution)/shard_map/ppermute | solution.py:960
  75.8 25.1 %collective-permute-start.11 = (bf16[3,704,128]{2,1,0:T(8,128)(2,1)S(1)}, bf16[3,704,128]{2,1,0:T(8,128)(2,1)S(1)}, u32[]{:S(2)}, u32[]{:S(2)}) collective-permute-start(bf16[3,704,128]{2,1,0:T(8,128)(2,1)S(1)} %pad_maximum_fusion.8), channel_id=1, source_target_pairs={{2,1},{1,2},{6,5},{5,6},{10,9},{9,10},{14,13},{13,14},{18,17},{17,... | collective-permute-start | bytes 1622024 | tf_op jit(solution)/shard_map/ppermute | solution.py:961
  76.8 23.6 %collective-permute-start.12 = (bf16[128,2048]{0,1:T(8,128)(2,1)S(1)}, bf16[128,2048]{0,1:T(8,128)(2,1)S(1)}, u32[]{:S(2)}, u32[]{:S(2)}) collective-permute-start(bf16[128,2048]{0,1:T(8,128)(2,1)S(1)} %pad_maximum_fusion.9), channel_id=1, source_target_pairs={{0,8},{4,12},{8,0},{12,4},{16,24},{20,28},{24,16},{28,20},{1,9},{5... | collective-permute-start | bytes 1572872 | tf_op jit(solution)/shard_map/ppermute | solution.py:728
  78.3 22.5 %collective-permute-start.13 = (bf16[128,2048]{0,1:T(8,128)(2,1)S(1)}, bf16[128,2048]{0,1:T(8,128)(2,1)S(1)}, u32[]{:S(2)}, u32[]{:S(2)}) collective-permute-start(bf16[128,2048]{0,1:T(8,128)(2,1)S(1)} %pad_maximum_fusion.9), channel_id=1, source_target_pairs={{0,16},{4,20},{8,24},{12,28},{16,0},{20,4},{24,8},{28,12},{1,17},{... | collective-permute-start | bytes 1572872 | tf_op jit(solution)/shard_map/ppermute | solution.py:728
  102.2 47.6 %collective-permute-start.22 = (bf16[128,2048]{0,1:T(8,128)(2,1)S(1)}, bf16[128,2048]{0,1:T(8,128)(2,1)S(1)}, u32[]{:S(2)}, u32[]{:S(2)}) collective-permute-start(bf16[128,2048]{0,1:T(8,128)(2,1)S(1)} %pad_maximum_fusion.9), channel_id=1, source_target_pairs={{0,4},{4,0},{8,12},{12,8},{16,20},{20,16},{24,28},{28,24},{1,5},{5... | collective-permute-start | bytes 1572872 | tf_op jit(solution)/shard_map/ppermute | solution.py:728
  124.4 22.9 %collective-permute-start.20 = (bf16[256,512]{1,0:T(8,128)(2,1)S(1)}, bf16[256,512]{1,0:T(8,128)(2,1)S(1)}, u32[]{:S(2)}, u32[]{:S(2)}) collective-permute-start(bf16[256,512]{1,0:T(8,128)(2,1)S(1)} %get-tuple-element.350), channel_id=1, source_target_pairs={{0,2},{1,3},{2,0},{3,1},{4,6},{5,7},{6,4},{7,5},{8,10},{9,11},{10,... | collective-permute-start | bytes 786440 | tf_op jit(solution)/shard_map/ppermute | solution.py:794
  124.5 22.8 %collective-permute-start.21 = (bf16[256,512]{1,0:T(8,128)(2,1)S(1)}, bf16[256,512]{1,0:T(8,128)(2,1)S(1)}, u32[]{:S(2)}, u32[]{:S(2)}) collective-permute-start(bf16[256,512]{1,0:T(8,128)(2,1)S(1)} %get-tuple-element.349), channel_id=1, source_target_pairs={{0,1},{1,2},{2,3},{3,0},{4,5},{5,6},{6,7},{7,4},{8,9},{9,10},{10,1... | collective-permute-start | bytes 786440 | tf_op jit(solution)/shard_map/ppermute | solution.py:794
  126.9 41.3 %collective-permute-start.30 = (bf16[2,3,704,128]{3,2,1,0:T(8,128)(2,1)S(1)}, bf16[2,3,704,128]{3,2,1,0:T(8,128)(2,1)}, u32[]{:S(2)}, u32[]{:S(2)}) collective-permute-start(bf16[2,3,704,128]{3,2,1,0:T(8,128)(2,1)S(1)} %pad_maximum_fusion.1.refs_8_), channel_id=1, source_target_pairs={{0,16},{4,20},{8,24},{12,28},{16,0},{20,4},{24,8},{28,12},{1,17},{... | collective-permute-start | bytes 3244040 | tf_op jit(solution)/shard_map/ppermute | solution.py:728
  131.3 36.9 %collective-permute-start.31 = (bf16[2,3,704,128]{3,2,1,0:T(8,128)(2,1)}, bf16[2,3,704,128]{3,2,1,0:T(8,128)(2,1)}, u32[]{:S(2)}, u32[]{:S(2)}) collective-permute-start(bf16[2,3,704,128]{3,2,1,0:T(8,128)(2,1)} %pad_maximum_fusion.2.refs_10_), channel_id=1, source_target_pairs={{0,8},{4,12},{8,0},{12,4},{16,24},{20,28},{24,16},{28,20},{1,9},{5... | collective-permute-start | bytes 3244040 | tf_op jit(solution)/shard_map/ppermute | solution.py:728
  208.4 25.1 %collective-permute-start.38 = (bf16[2,3,704,128]{3,2,1,0:T(8,128)(2,1)S(1)}, bf16[2,3,704,128]{3,2,1,0:T(8,128)(2,1)S(1)}, u32[]{:S(2)}, u32[]{:S(2)}) collective-permute-start(bf16[2,3,704,128]{3,2,1,0:T(8,128)(2,1)S(1)} %pad_maximum_fusion.3), channel_id=1, source_target_pairs={{0,8},{4,12},{8,0},{12,4},{16,24},{20,28},{24,16},{28,20},{1,9},{5... | collective-permute-start | bytes 3244040 | tf_op jit(solution)/shard_map/ppermute | solution.py:728
  209.1 24.9 %collective-permute-start.39 = (bf16[2,3,704,128]{3,2,1,0:T(8,128)(2,1)S(1)}, bf16[2,3,704,128]{3,2,1,0:T(8,128)(2,1)S(1)}, u32[]{:S(2)}, u32[]{:S(2)}) collective-permute-start(bf16[2,3,704,128]{3,2,1,0:T(8,128)(2,1)S(1)} %slice.212), channel_id=1, source_target_pairs={{0,16},{4,20},{8,24},{12,28},{16,0},{20,4},{24,8},{28,12},{1,17},{... | collective-permute-start | bytes 3244040 | tf_op jit(solution)/shard_map/ppermute | solution.py:728
  214.8 24.4 %collective-permute-start.35 = (bf16[256,512]{1,0:T(8,128)(2,1)S(1)}, bf16[256,512]{1,0:T(8,128)(2,1)S(1)}, u32[]{:S(2)}, u32[]{:S(2)}) collective-permute-start(bf16[256,512]{1,0:T(8,128)(2,1)S(1)} %get-tuple-element.347), channel_id=1, source_target_pairs={{0,1},{1,2},{2,3},{3,0},{4,5},{5,6},{6,7},{7,4},{8,9},{9,10},{10,1... | collective-permute-start | bytes 786440 | tf_op jit(solution)/shard_map/ppermute | solution.py:794
  215.2 24.0 %collective-permute-start.36 = (bf16[256,512]{1,0:T(8,128)(2,1)S(1)}, bf16[256,512]{1,0:T(8,128)(2,1)S(1)}, u32[]{:S(2)}, u32[]{:S(2)}) collective-permute-start(bf16[256,512]{1,0:T(8,128)(2,1)S(1)} %get-tuple-element.346), channel_id=1, source_target_pairs={{0,2},{1,3},{2,0},{3,1},{4,6},{5,7},{6,4},{7,5},{8,10},{9,11},{10,... | collective-permute-start | bytes 786440 | tf_op jit(solution)/shard_map/ppermute | solution.py:794
  234.0 27.7 %collective-permute-start.41 = (bf16[256,1024]{1,0:T(8,128)(2,1)}, bf16[256,1024]{1,0:T(8,128)(2,1)}, u32[]{:S(2)}, u32[]{:S(2)}) collective-permute-start(bf16[256,1024]{1,0:T(8,128)(2,1)} %get-tuple-element.230), channel_id=1, source_target_pairs={{0,4},{4,0},{8,12},{12,8},{16,20},{20,16},{24,28},{28,24},{1,5},{5... | collective-permute-start | bytes 1572872 | tf_op jit(solution)/shard_map/ppermute | solution.py:728
  238.1 25.0 %collective-permute-start.45 = (bf16[512,2048]{1,0:T(8,128)(2,1)}, bf16[512,2048]{1,0:T(8,128)(2,1)}, u32[]{:S(2)}, u32[]{:S(2)}) collective-permute-start(bf16[512,2048]{1,0:T(8,128)(2,1)} %convolution_convert_fusion), channel_id=1, source_target_pairs={{0,4},{4,0},{8,12},{12,8},{16,20},{20,16},{24,28},{28,24},{1,5},{5... | collective-permute-start | bytes 6291464 | tf_op jit(solution)/shard_map/ppermute | solution.py:728
  239.2 23.9 %collective-permute-start.42 = (bf16[256,1024]{1,0:T(8,128)(2,1)}, bf16[256,1024]{1,0:T(8,128)(2,1)}, u32[]{:S(2)}, u32[]{:S(2)}) collective-permute-start(bf16[256,1024]{1,0:T(8,128)(2,1)} %add_convert_fusion.8), channel_id=1, source_target_pairs={{0,1},{1,0},{2,3},{3,2},{4,5},{5,4},{6,7},{7,6},{8,9},{9,8},{10,11... | collective-permute-start | bytes 1572872 | tf_op jit(solution)/shard_map/ppermute | solution.py:728
  269.0 24.7 %collective-permute-start.49 = (bf16[128,2048]{1,0:T(8,128)(2,1)}, bf16[128,2048]{1,0:T(8,128)(2,1)}, u32[]{:S(2)}, u32[]{:S(2)}) collective-permute-start(bf16[128,2048]{1,0:T(8,128)(2,1)} %get-tuple-element.327), channel_id=1, source_target_pairs={{0,8},{4,12},{8,0},{12,4},{16,24},{20,28},{24,16},{28,20},{1,9},{5... | collective-permute-start | bytes 1572872 | tf_op jit(solution)/shard_map/ppermute | solution.py:728
  269.6 25.6 %collective-permute-start.50 = (bf16[128,2048]{1,0:T(8,128)(2,1)}, bf16[128,2048]{1,0:T(8,128)(2,1)}, u32[]{:S(2)}, u32[]{:S(2)}) collective-permute-start(bf16[128,2048]{1,0:T(8,128)(2,1)} %get-tuple-element.326), channel_id=1, source_target_pairs={{0,16},{4,20},{8,24},{12,28},{16,0},{20,4},{24,8},{28,12},{1,17},{... | collective-permute-start | bytes 1572872 | tf_op jit(solution)/shard_map/ppermute | solution.py:728
  270.4 24.8 %collective-permute-start.51 = (bf16[128,2048]{1,0:T(8,128)(2,1)}, bf16[128,2048]{1,0:T(8,128)(2,1)}, u32[]{:S(2)}, u32[]{:S(2)}) collective-permute-start(bf16[128,2048]{1,0:T(8,128)(2,1)} %get-tuple-element.325), channel_id=1, source_target_pairs={{0,24},{4,28},{8,16},{12,20},{16,8},{20,12},{24,0},{28,4},{1,25},{... | collective-permute-start | bytes 1572872 | tf_op jit(solution)/shard_map/ppermute | solution.py:728
  (128 other events, 1268.0 us)
Sparse Core Ops, SparseCore 0:
  11.9 36.1 all-gather.1
  304.6 48.0 reduce-scatter.1

commit v3 on v2

--- a/solution.py
+++ b/solution.py
@@ -667,13 +667,22 @@
 
     rows = jnp.concatenate([ref[...] for ref in rows_refs], 0)
     cot = jnp.concatenate([ref[...] for ref in cot_refs], 0)
-    lanes = rows.shape[1] // len(out_refs)
+    piece = pl.program_id(0)
+    lanes = rows.shape[1] // 2
     for i, right in enumerate((rows, rows, cot)):
         grad = lax.dot_general(
             flipped_ref[i], right, (NN, ((), ())), preferred_element_type=f32
         ).astype(bf16)
-        for j, out_ref in enumerate(out_refs):
-            out_ref[0, i] = grad[:, j * lanes : (j + 1) * lanes]
+        if len(out_refs) == 1:
+            out_refs[0][0, i] = grad
+            continue
+        for j, kept in enumerate((piece % 2 == 0, piece < 2)):
+            some = grad[:, j * lanes : (j + 1) * lanes]
+            for ref, here in ((out_refs[2 * j], kept), (out_refs[2 * j + 1], ~kept)):
+
+                @pl.when(here)
+                def _():
+                    ref[0, i] = some
 
 
 def ffn_weight_grads(place, rows, cot, gate, up, hidden, pieces, split):
@@ -683,6 +692,18 @@
     width = hidden.shape[1]
     size = d // pieces
     column = pl.BlockSpec((count, size), lambda p, place: (0, p ^ place[0]))
+    if split == 1:
+        places = [lambda p: p]
+        shape = (pieces, 3, width, size)
+    else:
+        places = [
+            lambda p: p // 2, lambda p: p // 2,
+            lambda p: jnp.minimum(p, 1), lambda p: jnp.maximum(p - 2, 0),
+        ]
+        shape = (pieces // 2, 3, width, size // 2)
+    out_specs = [
+        pl.BlockSpec((1,) + shape[1:], lambda p, place, at=at: (at(p), 0, 0, 0)) for at in places
+    ]
     full = pl.BlockSpec((total, width), lambda p, place: (0, 0))
     return pl.pallas_call(
         functools.partial(ffn_grads_body, runs),
@@ -690,12 +711,10 @@
             num_scalar_prefetch=1,
             grid=(pieces,),
             in_specs=[column] * (2 * runs) + [full] * 3,
-            out_specs=[
-                pl.BlockSpec((1, 3, width, size // split), lambda p, place: (p, 0, 0, 0))
-            ] * split,
+            out_specs=out_specs,
             scratch_shapes=[pltpu.VMEM((3, width, total), bf16)],
         ),
-        out_shape=[jax.ShapeDtypeStruct((pieces, 3, width, size // split), bf16)] * split,
+        out_shape=[jax.ShapeDtypeStruct(shape, bf16)] * len(out_specs),
         compiler_params=pltpu.CompilerParams(
             dimension_semantics=("arbitrary",), vmem_limit_bytes=BUDGET
         ),
@@ -1005,17 +1024,15 @@
         return exchange(far, "tensor", 1)
 
     def sum_start(self, grads):
-        self.grads = grads
-        low, high = grads
-        across_x = jnp.stack([low[1], low[3]])
-        self.near = exchange(across_x, "dp", 2), exchange(high[2:], "dp", 4)
+        self.stay = grads[0], grads[2]
+        self.near = exchange(grads[1], "dp", 2), exchange(grads[3], "dp", 4)
 
     def sum_step(self, done):
-        low, high = self.grads
+        low, high = self.stay
         came = after(self.near, done)
         add = lambda x, y: (x.astype(f32) + y.astype(f32)).astype(bf16)
         self.kept = add(low[0], came[0][0]), add(high[0], came[1][0])
-        return add(low[2], came[0][1]), add(high[1], came[1][1])
+        return add(low[1], came[0][1]), add(high[1], came[1][1])
 
     def sum_far(self, sent):
         self.far = exchange(sent[0], "dp", 4), exchange(sent[1], "dp", 2)

time: 387 us -> 390 us (level)
  Pallas kernels: 86.6 us -> 91.8 us
    pallas_call x1, Pallas kernels: 11 us -> 16.2 us  [ffn_weight_grads(): pl.pallas_call(functools.partial(ffn_grads_body, runs), grid_spec=pltpu.P...]
  transfers between devices with their start and end apart: 67 -> 67, of which waited for: 22 -> 21; matrix products, arithmetic and copies ran while one was open for 19% -> 18% of each run, Pallas kernels for 18% -> 19%
where the time goes in v3:
time: 390 us; the launch traced here: 385 us
  waiting for transfers between devices  94.6 us (24%)
  Pallas kernels  91.8 us (24%)
  starting transfers between devices  86.9 us (22%)
  local copies, waits for them, and re-layouts  38.6 us (10%)
  other arithmetic  29 us (7%)
  matrix products  28.7 us (7%)
  between operations  15.9 us (4%)
    ppermute x40, waiting for transfers between devices, exchange(): lax.ppermute(x, axis, [(i, i ^ bit) for i in range(lax.axis_size(axis))])  51.3 us
    pallas_call x2, Pallas kernels, mixer_backward(): pl.pallas_call(functools.partial(backward_body, heads, prec), grid=(steps...  31 us
    ppermute x40, starting transfers between devices, exchange(): lax.ppermute(x, axis, [(i, i ^ bit) for i in range(lax.axis_size(axis))])  29.7 us
    ppermute x15, waiting for transfers between devices, shifted(): return lax.ppermute(x, axis, [(i, (i + by) % ways) for i in range(ways)])  28.9 us
    ppermute x15, starting transfers between devices, shifted(): return lax.ppermute(x, axis, [(i, (i + by) % ways) for i in range(ways)])  28.8 us
    dot_general x9, matrix products, product(): lax.dot_general(left, right, (dims, ((), ())), preferred_element_type=f32)  28.7 us
    pallas_call x2, Pallas kernels, mixer_forward(): pl.pallas_call(functools.partial(forward_body, heads, prec), grid=(steps,...  25.7 us
    ppermute x3, starting transfers between devices, line_gather(): below.append(lax.ppermute(below[-1], axis, up))  21.6 us
  transfers between devices with their start and end apart: 67, of which 21 were waited for; matrix products, arithmetic and copies ran while one was open for 18% of the time, Pallas kernels for 19%

profile of v3, /device:TPU:0, one launch (start us, length us, event | category | flops | bytes accessed | tf_op | source)
XLA Modules:
  0.0 385.4 jit_solution(930068142244603202)
XLA Ops:
  14.0 5.1 %collective-permute-start = (bf16[256,1024]{1,0:T(8,128)(2,1)S(1)}, bf16[256,1024]{1,0:T(8,128)(2,1)S(1)}, u32[]{:S(2)}, u32[]{:S(2)}) collective-permute-start(bf16[256,1024]{1,0:T(8,128)(2,1)S(1)} %fusion.8), channel_id=1, source_target_pairs={{0,1},{1,2},{2,3},{4,5},{5,6},{6,7},{8,9},{9,10},{10,11},{12,13},{... | collective-permute-start | bytes 1572872 | tf_op jit(solution)/shard_map/ppermute | solution.py:769
  20.4 5.4 %collective-permute-start.6 = (bf16[128,512]{0,1:T(8,128)(2,1)S(1)}, bf16[128,512]{0,1:T(8,128)(2,1)}, u32[]{:S(2)}, u32[]{:S(2)}) collective-permute-start(bf16[128,512]{0,1:T(8,128)(2,1)S(1)} %bitcast.124), channel_id=1, source_target_pairs={{0,3},{1,0},{2,1},{3,2},{4,7},{5,4},{6,5},{7,6},{8,11},{9,8},{10,9... | collective-permute-start | bytes 393224 | tf_op jit(solution)/shard_map/ppermute | solution.py:813
  27.1 4.2 %collective-permute-done = bf16[256,1024]{1,0:T(8,128)(2,1)S(1)} collective-permute-done((bf16[256,1024]{1,0:T(8,128)(2,1)S(1)}, bf16[256,1024]{1,0:T(8,128)(2,1)S(1)}, u32[]{:S(2)}, u32[]{:S(2)}) %collective-permute-start) | collective-permute-done | bytes 524320 | tf_op jit(solution)/shard_map/ppermute | solution.py:769
  31.3 9.5 %collective-permute-start.1 = (bf16[256,1024]{1,0:T(8,128)(2,1)S(1)}, bf16[256,1024]{1,0:T(8,128)(2,1)}, u32[]{:S(2)}, u32[]{:S(2)}) collective-permute-start(bf16[256,1024]{1,0:T(8,128)(2,1)S(1)} %collective-permute-done), channel_id=1, source_target_pairs={{0,1},{1,2},{2,3},{4,5},{5,6},{6,7},{8,9},{9,10},{10,11},{12,13},{... | collective-permute-start | bytes 1572872 | tf_op jit(solution)/shard_map/ppermute | solution.py:769
  44.2 4.0 %collective-permute-done.7 = bf16[128,512]{0,1:T(8,128)(2,1)} collective-permute-done((bf16[128,512]{0,1:T(8,128)(2,1)S(1)}, bf16[128,512]{0,1:T(8,128)(2,1)}, u32[]{:S(2)}, u32[]{:S(2)}) %collective-permute-start.7) | collective-permute-done | bytes 131104 | tf_op jit(solution)/shard_map/ppermute | solution.py:813
  49.9 7.0 %collective-permute-start.2 = (bf16[256,1024]{1,0:T(8,128)(2,1)}, bf16[256,1024]{1,0:T(8,128)(2,1)}, u32[]{:S(2)}, u32[]{:S(2)}) collective-permute-start(bf16[256,1024]{1,0:T(8,128)(2,1)} %collective-permute-done.1), channel_id=1, source_target_pairs={{0,1},{1,2},{2,3},{4,5},{5,6},{6,7},{8,9},{9,10},{10,11},{12,13},{... | collective-permute-start | bytes 1572872 | tf_op jit(solution)/shard_map/ppermute | solution.py:769
  62.3 4.5 %collective-permute-done.2 = bf16[256,1024]{1,0:T(8,128)(2,1)} collective-permute-done((bf16[256,1024]{1,0:T(8,128)(2,1)}, bf16[256,1024]{1,0:T(8,128)(2,1)}, u32[]{:S(2)}, u32[]{:S(2)}) %collective-permute-start.2) | collective-permute-done | bytes 524320 | tf_op jit(solution)/shard_map/ppermute | solution.py:769
  66.7 5.0 %collective-permute-done.5 = bf16[256,1024]{1,0:T(8,128)(2,1)} collective-permute-done((bf16[256,1024]{1,0:T(8,128)(2,1)}, bf16[256,1024]{1,0:T(8,128)(2,1)}, u32[]{:S(2)}, u32[]{:S(2)}) %collective-permute-start.5) | collective-permute-done | bytes 524320 | tf_op jit(solution)/shard_map/ppermute | solution.py:770
  80.9 5.9 %fusion.45.extra_ref.proj_ref = f32[1024,1664]{1,0:T(8,128)} fusion(bf16[1024,1024]{1,0:T(8,128)(2,1)S(1)} %pad_maximum_fusion, bf16[1024,1664]{1,0:T(8,128)(2,1)S(1)} %copy-done.66), kind=kOutput, calls=%fused_computation.168 | convolution fusion | flops 3489660928 | bytes 12320768 | tf_op jit(solution)/shard_map/dot_general | solution.py:739
  88.1 12.9 %mixer_forward.2 = (bf16[1024,512]{1,0:T(8,128)(2,1)}, f32[1024,1024]{1,0:T(8,128)}, f32[1024,512]{1,0:T(8,128)}, f32[1024,512]{1,0:T(8,128)}, f32[1024,256]{1,0...) custom-call(f32[1024,128]{1,0:T(8,128)} %pad.18.places_ref, ...), custom_call_target="tpu_custom_call" | custom-call | flops 65536000000 | bytes 12288000 | tf_op jit(solution)/shard_map/mixer_forward/pallas_call | solution.py:444
  108.0 12.9 %mixer_forward.3 = (bf16[1024,512]{1,0:T(8,128)(2,1)}, f32[1024,1024]{1,0:T(8,128)}, f32[1024,512]{1,0:T(8,128)}, f32[1024,512]{1,0:T(8,128)}, f32[1024,256]{1,0...) custom-call(f32[1024,128]{1,0:T(8,128)} %pad.18.places_ref, ...), custom_call_target="tpu_custom_call", output_to_operand_aliasing={{0}: (8, {}), {1}: (9, {}), {2}: (10, {}), {3}: (11, {}), {... | custom-call | flops 65536000000 | bytes 12288000 | tf_op jit(solution)/shard_map/mixer_forward/pallas_call | solution.py:444
  133.3 14.7 %collective-permute-done.20 = bf16[256,512]{1,0:T(8,128)(2,1)S(1)} collective-permute-done((bf16[256,512]{1,0:T(8,128)(2,1)S(1)}, bf16[256,512]{1,0:T(8,128)(2,1)S(1)}, u32[]{:S(2)}, u32[]{:S(2)}) %collective-permute-start.20) | collective-permute-done | bytes 262176 | tf_op jit(solution)/shard_map/ppermute | solution.py:813
  156.2 13.6 %collective-permute-done.27.refs_2_ = bf16[256,1024]{1,0:T(8,128)(2,1)} collective-permute-done((bf16[256,1024]{1,0:T(8,128)(2,1)}, bf16[256,1024]{1,0:T(8,128)(2,1)}, u32[]{:S(2)}, u32[]{:S(2)}) %collective-permute-start.27) | collective-permute-done | bytes 524320 | tf_op jit(solution)/shard_map/ppermute | solution.py:747
  172.0 18.8 %ffn_both.1 = (bf16[1024,704]{1,0:T(8,128)(2,1)}, bf16[1024,704]{1,0:T(8,128)(2,1)}, bf16[1024,704]{1,0:T(8,128)(2,1)}, bf16[256,1024]{1,0:T(8,128)(2,1)}, bf16[...) custom-call(s32[1]{0:T(128)} %bitcast.34.place_ref, ...), custom_call_target="tpu_custom_call" | custom-call | flops 17716740096 | bytes 8388608 | tf_op jit(solution)/shard_map/ffn_both/pallas_call | solution.py:634
  194.9 16.2 %ffn_weight_grads.1 = (bf16[2,3,704,128]{3,2,1,0:T(8,128)(2,1)}, bf16[2,3,704,128]{3,2,1,0:T(8,128)(2,1)}, bf16[2,3,704,128]{3,2,1,0:T(8,128)(2,1)}, bf16[2,3,704,128]{3,2,1,0:T(8,128)(2,1)}) custom-call(s32[1]{0:T(128)} %bitcast.34.place_ref, bf16[256,1024]{1,0:T(8,128)(2,1)} %multiply_convert_fusion.refs_0_, ...), custom_call_target="tpu_custom_call" | custom-call | flops 8858370048 | bytes 8388608 | tf_op jit(solution)/shard_map/ffn_weight_grads/pallas_call | solution.py:708
  222.6 14.5 %collective-permute-done.38 = bf16[2,3,704,128]{3,2,1,0:T(8,128)(2,1)S(1)} collective-permute-done((bf16[2,3,704,128]{3,2,1,0:T(8,128)(2,1)}, bf16[2,3,704,128]{3,2,1,0:T(8,128)(2,1)S(1)}, u32[]{:S(2)}, u32[]{:S(2)}) %collective-permute-start.38) | collective-permute-done | bytes 1081376 | tf_op jit(solution)/shard_map/ppermute | solution.py:747
  250.2 15.5 %mixer_backward.2 = (bf16[1024,1664]{1,0:T(8,128)(2,1)}, f32[2,128,256]{2,1,0:T(8,128)}, f32[8,1024]{1,0:T(8,128)}, f32[4,1024]{1,0:T(4,128)}, f32[8,128]{1,0:T(8,128)}, /*index=5*/f32[1,512]{1,0:T(1,128)}) custom-call(f32[1024,128]{1,0:T(8,128)} %pad.18.places_ref, f32[1024,1664]{1,0:T(8,128)} %fusion.45.extra_ref.proj_ref, ...), custom_call_target="tpu_custom_call" | custom-call | flops 98304000000 | bytes 14336000 | tf_op jit(solution)/shard_map/mixer_backward/pallas_call | solution.py:499
  279.2 15.5 %mixer_backward.3 = (bf16[1024,1664]{1,0:T(8,128)(2,1)}, f32[2,128,256]{2,1,0:T(8,128)}, f32[8,1024]{1,0:T(8,128)}, f32[4,1024]{1,0:T(4,128)}, f32[8,128]{1,0:T(8,128)}, /*index=5*/f32[1,512]{1,0:T(1,128)}) custom-call(f32[1024,128]{1,0:T(8,128)} %pad.18.places_ref, f32[1024,1664]{1,0:T(8,128)} %fusion.45.extra_ref.proj_ref, ...), custom_call_target="tpu_custom_call", output_to_operand_aliasing={{0}: (20, {})} | custom-call | flops 98304000000 | bytes 14336000 | tf_op jit(solution)/shard_map/mixer_backward/pallas_call | solution.py:499
  298.6 8.3 %convolution_convert_fusion.3 = bf16[1024,1024]{1,0:T(8,128)(2,1)} fusion(bf16[1024,1664]{1,0:T(8,128)(2,1)} %get-tuple-element.265, bf16[1024,1664]{1,0:T(8,128)(2,1)} %all-gather.2.cloned.1.call-done), kind=kOutput, calls=%fused_computation.10 | convolution fusion | flops 3490709504 | bytes 8912896 | tf_op jit(solution)/shard_map/dot_general | solution.py:739
  312.8 3.9 %convolution_convert_fusion.1 = bf16[512,1536]{1,0:T(8,128)(2,1)S(1)} fusion(bf16[1024,1664]{1,0:T(8,128)(2,1)} %get-tuple-element.265, pred[]{:T(512)S(6)} %eq.69, bf16[1024,128]{1,0:T(8,128)(2,1)S(1)} %copy-done.42, bf16[1024,128]{1,0:T(8,128)(2,1)S(1)} %copy-done.43, bf16[1024,128]{1,0:T(8,128)(2,1)S(1)} %copy-done.44, ...), kind=kOutput, calls=%fused_computation.4 | convolution fusion | flops 1620312064 | bytes 6815745 | tf_op jit(solution)/shard_map/dot_general | solution.py:739
  336.8 6.7 %collective-permute-done.56 = bf16[128,1536]{1,0:T(8,128)(2,1)S(1)} collective-permute-done((bf16[128,1536]{1,0:T(8,128)(2,1)}, bf16[128,1536]{1,0:T(8,128)(2,1)S(1)}, u32[]{:S(2)}, u32[]{:S(2)}) %collective-permute-start.56) | collective-permute-done | bytes 393248 | tf_op jit(solution)/shard_map/ppermute | solution.py:747
  343.5 7.3 %collective-permute-done.57 = bf16[128,1536]{1,0:T(8,128)(2,1)S(1)} collective-permute-done((bf16[128,1536]{1,0:T(8,128)(2,1)}, bf16[128,1536]{1,0:T(8,128)(2,1)S(1)}, u32[]{:S(2)}, u32[]{:S(2)}) %collective-permute-start.57) | collective-permute-done | bytes 393248 | tf_op jit(solution)/shard_map/ppermute | solution.py:747
  353.0 5.6 %collective-permute-start.60 = (f32[2064]{0:T(1024)S(1)}, f32[2064]{0:T(1024)S(1)}, u32[]{:S(2)}, u32[]{:S(2)}) collective-permute-start(f32[2064]{0:T(1024)S(1)} %slice.229), channel_id=1, source_target_pairs={{0,2},{1,3},{2,0},{3,1},{4,6},{5,7},{6,4},{7,5},{8,10},{9,11},{10,... | collective-permute-start | bytes 24776 | tf_op jit(solution)/shard_map/ppermute | solution.py:813
  369.1 4.5 %collective-permute-done.63 = bf16[128,512]{1,0:T(8,128)(2,1)S(1)} collective-permute-done((bf16[128,512]{1,0:T(8,128)(2,1)S(1)}, bf16[128,512]{1,0:T(8,128)(2,1)S(1)}, u32[]{:S(2)}, u32[]{:S(2)}) %collective-permute-start.63) | collective-permute-done | bytes 131104 | tf_op jit(solution)/shard_map/ppermute | solution.py:813
  (419 shorter events, 148.1 us)
Async XLA Ops:
  7.2 51.0 %all-gather.2.cloned.1.call-start = ((), (), s32[]{:S(2)}) async-start(), calls=%async_computation.1 | async-start | bytes 3833856 | tf_op jit(solution)/shard_map/all_gather | solution.py:1101
  11.8 362.8 %reduce-scatter.2.cloned.1.call-start = ((), (), s32[]{:S(2)}) async-start(), calls=%async_computation.2 | async-start | bytes 2621440 | tf_op jit(solution)/shard_map/reduce_scatter | solution.py:1216
  20.4 23.7 %collective-permute-start.6 = (bf16[128,512]{0,1:T(8,128)(2,1)S(1)}, bf16[128,512]{0,1:T(8,128)(2,1)}, u32[]{:S(2)}, u32[]{:S(2)}) collective-permute-start(bf16[128,512]{0,1:T(8,128)(2,1)S(1)} %bitcast.124), channel_id=1, source_target_pairs={{0,3},{1,0},{2,1},{3,2},{4,7},{5,4},{6,5},{7,6},{8,11},{9,8},{10,9... | collective-permute-start | bytes 393224 | tf_op jit(solution)/shard_map/ppermute | solution.py:813
  25.8 22.3 %collective-permute-start.7 = (bf16[128,512]{0,1:T(8,128)(2,1)S(1)}, bf16[128,512]{0,1:T(8,128)(2,1)}, u32[]{:S(2)}, u32[]{:S(2)}) collective-permute-start(bf16[128,512]{0,1:T(8,128)(2,1)S(1)} %bitcast.125), channel_id=1, source_target_pairs={{0,2},{1,3},{2,0},{3,1},{4,6},{5,7},{6,4},{7,5},{8,10},{9,11},{10,... | collective-permute-start | bytes 393224 | tf_op jit(solution)/shard_map/ppermute | solution.py:813
  75.1 26.3 %collective-permute-start.10 = (bf16[3,704,128]{2,1,0:T(8,128)(2,1)S(1)}, bf16[3,704,128]{2,1,0:T(8,128)(2,1)S(1)}, u32[]{:S(2)}, u32[]{:S(2)}) collective-permute-start(bf16[3,704,128]{2,1,0:T(8,128)(2,1)S(1)} %pad_maximum_fusion.7), channel_id=1, source_target_pairs={{1,0},{0,2},{2,3},{3,1},{5,4},{4,6},{6,7},{7,5},{9,8},{8,10},{10,1... | collective-permute-start | bytes 1622024 | tf_op jit(solution)/shard_map/ppermute | solution.py:979
  76.4 25.0 %collective-permute-start.11 = (bf16[3,704,128]{2,1,0:T(8,128)(2,1)S(1)}, bf16[3,704,128]{2,1,0:T(8,128)(2,1)S(1)}, u32[]{:S(2)}, u32[]{:S(2)}) collective-permute-start(bf16[3,704,128]{2,1,0:T(8,128)(2,1)S(1)} %pad_maximum_fusion.7), channel_id=1, source_target_pairs={{2,1},{1,2},{6,5},{5,6},{10,9},{9,10},{14,13},{13,14},{18,17},{17,... | collective-permute-start | bytes 1622024 | tf_op jit(solution)/shard_map/ppermute | solution.py:980
  77.3 23.6 %collective-permute-start.12 = (bf16[128,2048]{0,1:T(8,128)(2,1)S(1)}, bf16[128,2048]{0,1:T(8,128)(2,1)S(1)}, u32[]{:S(2)}, u32[]{:S(2)}) collective-permute-start(bf16[128,2048]{0,1:T(8,128)(2,1)S(1)} %pad_maximum_fusion.8), channel_id=1, source_target_pairs={{0,8},{4,12},{8,0},{12,4},{16,24},{20,28},{24,16},{28,20},{1,9},{5... | collective-permute-start | bytes 1572872 | tf_op jit(solution)/shard_map/ppermute | solution.py:747
  78.9 22.5 %collective-permute-start.13 = (bf16[128,2048]{0,1:T(8,128)(2,1)S(1)}, bf16[128,2048]{0,1:T(8,128)(2,1)S(1)}, u32[]{:S(2)}, u32[]{:S(2)}) collective-permute-start(bf16[128,2048]{0,1:T(8,128)(2,1)S(1)} %pad_maximum_fusion.8), channel_id=1, source_target_pairs={{0,16},{4,20},{8,24},{12,28},{16,0},{20,4},{24,8},{28,12},{1,17},{... | collective-permute-start | bytes 1572872 | tf_op jit(solution)/shard_map/ppermute | solution.py:747
  102.7 47.7 %collective-permute-start.22 = (bf16[128,2048]{0,1:T(8,128)(2,1)S(1)}, bf16[128,2048]{0,1:T(8,128)(2,1)S(1)}, u32[]{:S(2)}, u32[]{:S(2)}) collective-permute-start(bf16[128,2048]{0,1:T(8,128)(2,1)S(1)} %pad_maximum_fusion.8), channel_id=1, source_target_pairs={{0,4},{4,0},{8,12},{12,8},{16,20},{20,16},{24,28},{28,24},{1,5},{5... | collective-permute-start | bytes 1572872 | tf_op jit(solution)/shard_map/ppermute | solution.py:747
  125.1 22.9 %collective-permute-start.20 = (bf16[256,512]{1,0:T(8,128)(2,1)S(1)}, bf16[256,512]{1,0:T(8,128)(2,1)S(1)}, u32[]{:S(2)}, u32[]{:S(2)}) collective-permute-start(bf16[256,512]{1,0:T(8,128)(2,1)S(1)} %get-tuple-element.356), channel_id=1, source_target_pairs={{0,2},{1,3},{2,0},{3,1},{4,6},{5,7},{6,4},{7,5},{8,10},{9,11},{10,... | collective-permute-start | bytes 786440 | tf_op jit(solution)/shard_map/ppermute | solution.py:813
  125.1 22.8 %collective-permute-start.21 = (bf16[256,512]{1,0:T(8,128)(2,1)S(1)}, bf16[256,512]{1,0:T(8,128)(2,1)S(1)}, u32[]{:S(2)}, u32[]{:S(2)}) collective-permute-start(bf16[256,512]{1,0:T(8,128)(2,1)S(1)} %get-tuple-element.355), channel_id=1, source_target_pairs={{0,1},{1,2},{2,3},{3,0},{4,5},{5,6},{6,7},{7,4},{8,9},{9,10},{10,1... | collective-permute-start | bytes 786440 | tf_op jit(solution)/shard_map/ppermute | solution.py:813
  127.6 42.2 %collective-permute-start.30 = (bf16[2,3,704,128]{3,2,1,0:T(8,128)(2,1)S(1)}, bf16[2,3,704,128]{3,2,1,0:T(8,128)(2,1)}, u32[]{:S(2)}, u32[]{:S(2)}) collective-permute-start(bf16[2,3,704,128]{3,2,1,0:T(8,128)(2,1)S(1)} %pad_maximum_fusion.1.refs_8_), channel_id=1, source_target_pairs={{0,16},{4,20},{8,24},{12,28},{16,0},{20,4},{24,8},{28,12},{1,17},{... | collective-permute-start | bytes 3244040 | tf_op jit(solution)/shard_map/ppermute | solution.py:747
  132.0 37.8 %collective-permute-start.31 = (bf16[2,3,704,128]{3,2,1,0:T(8,128)(2,1)S(1)}, bf16[2,3,704,128]{3,2,1,0:T(8,128)(2,1)}, u32[]{:S(2)}, u32[]{:S(2)}) collective-permute-start(bf16[2,3,704,128]{3,2,1,0:T(8,128)(2,1)S(1)} %pad_maximum_fusion.2.refs_10_), channel_id=1, source_target_pairs={{0,8},{4,12},{8,0},{12,4},{16,24},{20,28},{24,16},{28,20},{1,9},{5... | collective-permute-start | bytes 3244040 | tf_op jit(solution)/shard_map/ppermute | solution.py:747
  211.2 25.9 %collective-permute-start.38 = (bf16[2,3,704,128]{3,2,1,0:T(8,128)(2,1)}, bf16[2,3,704,128]{3,2,1,0:T(8,128)(2,1)S(1)}, u32[]{:S(2)}, u32[]{:S(2)}) collective-permute-start(bf16[2,3,704,128]{3,2,1,0:T(8,128)(2,1)} %get-tuple-element.218), channel_id=1, source_target_pairs={{0,8},{4,12},{8,0},{12,4},{16,24},{20,28},{24,16},{28,20},{1,9},{5... | collective-permute-start | bytes 3244040 | tf_op jit(solution)/shard_map/ppermute | solution.py:747
  211.8 25.6 %collective-permute-start.39 = (bf16[2,3,704,128]{3,2,1,0:T(8,128)(2,1)}, bf16[2,3,704,128]{3,2,1,0:T(8,128)(2,1)S(1)}, u32[]{:S(2)}, u32[]{:S(2)}) collective-permute-start(bf16[2,3,704,128]{3,2,1,0:T(8,128)(2,1)} %get-tuple-element.219), channel_id=1, source_target_pairs={{0,16},{4,20},{8,24},{12,28},{16,0},{20,4},{24,8},{28,12},{1,17},{... | collective-permute-start | bytes 3244040 | tf_op jit(solution)/shard_map/ppermute | solution.py:747
  217.4 25.5 %collective-permute-start.35 = (bf16[256,512]{1,0:T(8,128)(2,1)S(1)}, bf16[256,512]{1,0:T(8,128)(2,1)S(1)}, u32[]{:S(2)}, u32[]{:S(2)}) collective-permute-start(bf16[256,512]{1,0:T(8,128)(2,1)S(1)} %get-tuple-element.353), channel_id=1, source_target_pairs={{0,1},{1,2},{2,3},{3,0},{4,5},{5,6},{6,7},{7,4},{8,9},{9,10},{10,1... | collective-permute-start | bytes 786440 | tf_op jit(solution)/shard_map/ppermute | solution.py:813
  219.1 23.7 %collective-permute-start.36 = (bf16[256,512]{1,0:T(8,128)(2,1)S(1)}, bf16[256,512]{1,0:T(8,128)(2,1)S(1)}, u32[]{:S(2)}, u32[]{:S(2)}) collective-permute-start(bf16[256,512]{1,0:T(8,128)(2,1)S(1)} %get-tuple-element.352), channel_id=1, source_target_pairs={{0,2},{1,3},{2,0},{3,1},{4,6},{5,7},{6,4},{7,5},{8,10},{9,11},{10,... | collective-permute-start | bytes 786440 | tf_op jit(solution)/shard_map/ppermute | solution.py:813
  237.3 28.4 %collective-permute-start.41 = (bf16[256,1024]{1,0:T(8,128)(2,1)}, bf16[256,1024]{1,0:T(8,128)(2,1)}, u32[]{:S(2)}, u32[]{:S(2)}) collective-permute-start(bf16[256,1024]{1,0:T(8,128)(2,1)} %get-tuple-element.238), channel_id=1, source_target_pairs={{0,4},{4,0},{8,12},{12,8},{16,20},{20,16},{24,28},{28,24},{1,5},{5... | collective-permute-start | bytes 1572872 | tf_op jit(solution)/shard_map/ppermute | solution.py:747
  241.1 26.0 %collective-permute-start.45 = (bf16[512,2048]{1,0:T(8,128)(2,1)}, bf16[512,2048]{1,0:T(8,128)(2,1)}, u32[]{:S(2)}, u32[]{:S(2)}) collective-permute-start(bf16[512,2048]{1,0:T(8,128)(2,1)} %convolution_convert_fusion), channel_id=1, source_target_pairs={{0,4},{4,0},{8,12},{12,8},{16,20},{20,16},{24,28},{28,24},{1,5},{5... | collective-permute-start | bytes 6291464 | tf_op jit(solution)/shard_map/ppermute | solution.py:747
  242.8 24.2 %collective-permute-start.42 = (bf16[256,1024]{1,0:T(8,128)(2,1)}, bf16[256,1024]{1,0:T(8,128)(2,1)}, u32[]{:S(2)}, u32[]{:S(2)}) collective-permute-start(bf16[256,1024]{1,0:T(8,128)(2,1)} %add_convert_fusion.8), channel_id=1, source_target_pairs={{0,1},{1,0},{2,3},{3,2},{4,5},{5,4},{6,7},{7,6},{8,9},{9,8},{10,11... | collective-permute-start | bytes 1572872 | tf_op jit(solution)/shard_map/ppermute | solution.py:747
  244.5 22.6 %collective-permute-start.43 = (bf16[3,704,128]{2,1,0:T(8,128)(2,1)S(1)}, bf16[3,704,128]{2,1,0:T(8,128)(2,1)S(1)}, u32[]{:S(2)}, u32[]{:S(2)}) collective-permute-start(bf16[3,704,128]{2,1,0:T(8,128)(2,1)S(1)} %get-tuple-element.240), channel_id=1, source_target_pairs={{0,16},{4,20},{8,24},{12,28},{16,0},{20,4},{24,8},{28,12},{1,17},{... | collective-permute-start | bytes 1622024 | tf_op jit(solution)/shard_map/ppermute | solution.py:747
  271.9 24.7 %collective-permute-start.49 = (bf16[128,2048]{1,0:T(8,128)(2,1)}, bf16[128,2048]{1,0:T(8,128)(2,1)}, u32[]{:S(2)}, u32[]{:S(2)}) collective-permute-start(bf16[128,2048]{1,0:T(8,128)(2,1)} %get-tuple-element.333), channel_id=1, source_target_pairs={{0,8},{4,12},{8,0},{12,4},{16,24},{20,28},{24,16},{28,20},{1,9},{5... | collective-permute-start | bytes 1572872 | tf_op jit(solution)/shard_map/ppermute | solution.py:747
  272.4 24.1 %collective-permute-start.50 = (bf16[128,2048]{1,0:T(8,128)(2,1)}, bf16[128,2048]{1,0:T(8,128)(2,1)}, u32[]{:S(2)}, u32[]{:S(2)}) collective-permute-start(bf16[128,2048]{1,0:T(8,128)(2,1)} %get-tuple-element.332), channel_id=1, source_target_pairs={{0,16},{4,20},{8,24},{12,28},{16,0},{20,4},{24,8},{28,12},{1,17},{... | collective-permute-start | bytes 1572872 | tf_op jit(solution)/shard_map/ppermute | solution.py:747
  273.2 24.3 %collective-permute-start.51 = (bf16[128,2048]{1,0:T(8,128)(2,1)S(1)}, bf16[128,2048]{1,0:T(8,128)(2,1)}, u32[]{:S(2)}, u32[]{:S(2)}) collective-permute-start(bf16[128,2048]{1,0:T(8,128)(2,1)S(1)} %get-tuple-element.331), channel_id=1, source_target_pairs={{0,24},{4,28},{8,16},{12,20},{16,8},{20,12},{24,0},{28,4},{1,25},{... | collective-permute-start | bytes 1572872 | tf_op jit(solution)/shard_map/ppermute | solution.py:747
  (128 other events, 1220.4 us)
Sparse Core Ops, SparseCore 0:
  11.9 36.1 all-gather.1
  307.1 47.7 reduce-scatter.1
